TPU v7x, 32 devices: a whole 2x2x4 slice. The times are simulated.
32 devices in a mesh: gx: 8 (over y, x, core), ao: 4 (over z).
Axes of the slice: x: 2, y: 2, z: 4, core: 2. Of those that a mesh axis runs over, the one named last changes fastest.
Arguments:
- density: bfloat16 [384, 128, 1024], P('ao', 'gx'), may hold values from 0 to 2
- kernel: bfloat16 [384, 384], replicated, may hold values from -0.0102062073 to 0.0102062073
- neighbours: int32 [384, 6], replicated, may hold values from 0 to 383, as said below
- weights: int32 [384, 6], replicated, may hold values from 1 to 3
- signs: int32 [2, 384], replicated, may hold values from 0 to 1
- speeds: float32 [2, 384], replicated, may hold values from 0.05 to 0.2
Outputs:
- evolved: bfloat16 [384, 128, 1024], P('ao', 'gx')
Inputs may be any that keep to these rules, and one draw needn't show every extreme that they name: `neighbours`: each entry names an orientation other than its own row's.
All inputs are finite; a program needn't handle non-finite values.
Results may differ from a plain program's by a relative error of at most 0.0052.
Values may be sent and summed in bfloat16 or wider, within the bound.
No kernel may reach another device: no remote copies, remote signals or barrier semaphores. Data moves between devices by JAX's collectives and lax.ppermute only.
A program may use at most 128 MiB of HBM per device.

v0:
```python
import jax
import jax.numpy as jnp
from jax import lax
from jax.sharding import PartitionSpec as P

TIME_STEPS = 3


rotation_rate = 0.05


def extended(value, sides, width):
    for axis, dim in sides:
        devices, length = (lax.axis_size(axis), value.shape[dim])
        up = [(i, (i + 1) % devices) for i in range(devices)]
        down = [(j, i) for i, j in up]
        last = lax.slice_in_dim(value, length - width, length, axis=dim)
        leading = lax.slice_in_dim(value, 0, width, axis=dim)
        before = lax.ppermute(last, axis, up)
        after = lax.ppermute(leading, axis, down)
        value = jnp.concatenate([before, value, after], axis=dim)
    return value


def upwind(centre, behind_one, behind_two, ahead_one, ahead_two, direction, speed):
    rear = 0.5 * (3.0 * centre - 4.0 * behind_one + behind_two)
    front = 0.5 * (3.0 * centre - 4.0 * ahead_one + ahead_two)
    return speed * jnp.where(direction == 1, rear, front)


def stencil_matrix(neighbours, weights):
    number = neighbours.shape[0]
    labels = jnp.arange(number, dtype=jnp.int32)
    matches = (neighbours[:, :, None] == labels[None, None, :]).astype(jnp.float32)
    scaled = weights.astype(jnp.float32)
    coupled = jnp.sum(scaled[:, :, None] * matches, axis=1)
    totals = jnp.sum(scaled, axis=1)
    identity = (labels[:, None] == labels[None, :]).astype(jnp.float32)
    return (coupled - totals[:, None] * identity).astype(jnp.bfloat16)


def rotate_block(block, kernel, turn_matrix):
    block_shape = block.shape
    values = block.reshape(block_shape[0], -1)
    potential = jnp.dot(kernel, values, preferred_element_type=jnp.float32)
    wide_values = values.astype(jnp.float32)
    drifted = (wide_values * (1.0 + potential)).astype(jnp.bfloat16)
    turned = jnp.dot(turn_matrix, drifted, preferred_element_type=jnp.float32)
    return (wide_values + rotation_rate * turned).astype(jnp.bfloat16).reshape(block_shape)


def per_device(density, kernel, neighbours, weights, signs, speeds):
    turn_matrix = stencil_matrix(neighbours, weights)
    share = density.shape[0]
    offset = lax.axis_index("ao") * share
    local_signs = lax.dynamic_slice_in_dim(signs, offset, share, 1)
    local_speeds = lax.dynamic_slice_in_dim(speeds, offset, share, 1)
    current = density
    for section_index in range(TIME_STEPS):
        widened = extended(current, (("gx", 1),), 2).astype(jnp.float32)
        centre = current.astype(jnp.float32)
        along_rows = upwind(
            centre,
            widened[:, 1:-3],
            widened[:, :-4],
            widened[:, 3:-1],
            widened[:, 4:],
            local_signs[0][:, None, None],
            local_speeds[0][:, None, None],
        )
        along_columns = upwind(
            centre,
            jnp.roll(centre, 1, 2),
            jnp.roll(centre, 2, 2),
            jnp.roll(centre, -1, 2),
            jnp.roll(centre, -2, 2),
            local_signs[1][:, None, None],
            local_speeds[1][:, None, None],
        )
        advected = (centre - along_rows - along_columns).astype(jnp.bfloat16)
        current = lax.all_to_all(
            rotate_block(
                lax.all_to_all(advected, "ao", split_axis=2, concat_axis=0, tiled=True),
                kernel,
                turn_matrix,
            ),
            "ao",
            split_axis=0,
            concat_axis=2,
            tiled=True,
        )
    return current


def solution(mesh):
    in_specs = (P("ao", "gx", None), P(), P(), P(), P(), P())
    out_specs = P("ao", "gx", None)
    return jax.shard_map(
        per_device, mesh=mesh, in_specs=in_specs, out_specs=out_specs, check_vma=False
    )
```

profile of v0, /device:TPU:0, one launch (start us, length us, event | category | flops | bytes accessed | tf_op | source)
XLA Modules:
  0.0 750.1 jit_solution(2188474904337138584)
XLA Ops:
  10.3 6.2 fusion.66
  16.4 6.2 fusion.64
  30.7 14.4 %fusion.41 = bf16[96,16,1024]{2,1,0:T(8,128)(2,1)} fusion(f32[96,20,1024]{2,1,0:T(8,128)S(1)} %maximum_convert_fusion, f32[96,16,1023]{2,1,0:T(8,128)} %get-tuple-element.30, f32[96,16,1]{2,1,0:T(8,128)} %get-tuple-element.32, f32[96,16,1022]{2,1,0:T(8,128)} %get-tuple-element.26, f32[96,16,2]{2,1,0:T(8,128)} %get-tuple-element.28, ...), kind=kLoop, calls=%fused_computation.60 | loop fusion | flops 45613056 | bytes 56624064 | tf_op jit(solution)/shard_map/convert_element_type | solution.py:80
  45.1 7.2 copy.196
  59.4 91.6 %all-to-all-done = bf16[96,16,1024]{0,1,2:T(8,128)(2,1)} async-done(((bf16[96,16,1024]{0,1,2:T(8,128)(2,1)}), bf16[96,16,1024]{0,1,2:T(8,128)(2,1)}, u32[]{:S(2)}, u32[]{:S(2)}) %all-to-all-start) | async-done | bytes 3145760 | tf_op jit(solution)/shard_map/all_to_all | solution.py:83
  151.0 6.9 copy.197
  165.9 8.4 %fusion.1 = bf16[384,4096]{0,1:T(8,128)(2,1)} fusion(bf16[384,4096]{0,1:T(8,128)(2,1)} %copy.198, bf16[384,384]{1,0:T(8,128)(2,1)} %subtract_convert_fusion, bf16[384,4096]{1,0:T(8,128)(2,1)S(1)} %bitcast.86, bf16[384,384]{1,0:T(8,128)(2,1)S(1)} %copy-done), kind=kOutput, calls=%fused_computation.7 | convolution fusion | flops 2428502016 | bytes 10027008 | tf_op jit(solution)/shard_map/dot_general | solution.py:48
  178.4 72.7 %all_to_all.99 = bf16[384,16,256]{2,1,0:T(8,128)(2,1)S(1)} all-to-all(bf16[384,16,256]{2,1,0:T(8,128)(2,1)S(1)} %copy.200), channel_id=1, replica_groups=mesh['gx'=8,'ao'=4] {'ao'}, dimensions={0} | all-to-all | bytes 6291456 | tf_op jit(solution)/shard_map/all_to_all | solution.py:81
  257.2 6.2 fusion.59
  269.2 5.8 collective-permute-done.3
  279.4 14.5 %fusion.26 = bf16[96,16,1024]{2,1,0:T(8,128)(2,1)} fusion(f32[96,20,1024]{2,1,0:T(8,128)S(1)} %maximum_convert_fusion.1, f32[96,16,1023]{2,1,0:T(8,128)} %get-tuple-element.20, f32[96,16,1]{2,1,0:T(8,128)} %get-tuple-element.22, f32[96,16,1022]{2,1,0:T(8,128)} %get-tuple-element.16, f32[96,16,2]{2,1,0:T(8,128)} %get-tuple-element.18, ...), kind=kLoop, calls=%fused_computation.39 | loop fusion | flops 45613056 | bytes 56624064 | tf_op jit(solution)/shard_map/convert_element_type | solution.py:80
  293.8 7.1 copy.206
  301.0 96.9 %all_to_all.100 = bf16[96,16,1024]{0,1,2:T(8,128)(2,1)} all-to-all(bf16[96,16,1024]{0,1,2:T(8,128)(2,1)} %copy.206), channel_id=1, replica_groups=mesh['gx'=8,'ao'=4] {'ao'}, dimensions={2} | all-to-all | bytes 6291456 | tf_op jit(solution)/shard_map/all_to_all | solution.py:83
  397.8 6.9 copy.207
  412.7 8.4 %fusion.3 = bf16[384,4096]{0,1:T(8,128)(2,1)} fusion(bf16[384,4096]{0,1:T(8,128)(2,1)} %copy.208, bf16[384,384]{1,0:T(8,128)(2,1)} %subtract_convert_fusion, bf16[384,4096]{1,0:T(8,128)(2,1)S(1)} %bitcast.88, bf16[384,384]{1,0:T(8,128)(2,1)S(1)} %copy-done), kind=kOutput, calls=%fused_computation.9 | convolution fusion | flops 2428502016 | bytes 10027008 | tf_op jit(solution)/shard_map/dot_general | solution.py:48
  425.2 72.4 %all_to_all.101 = bf16[384,16,256]{2,1,0:T(8,128)(2,1)S(1)} all-to-all(bf16[384,16,256]{2,1,0:T(8,128)(2,1)S(1)} %copy.210), channel_id=1, replica_groups=mesh['gx'=8,'ao'=4] {'ao'}, dimensions={0} | all-to-all | bytes 6291456 | tf_op jit(solution)/shard_map/all_to_all | solution.py:81
  503.8 6.2 fusion.54
  516.3 6.2 collective-permute-done.5
  527.9 14.5 %fusion.11 = bf16[96,16,1024]{2,1,0:T(8,128)(2,1)} fusion(f32[96,20,1024]{2,1,0:T(8,128)S(1)} %maximum_convert_fusion.2, f32[96,16,1023]{2,1,0:T(8,128)} %get-tuple-element.10, f32[96,16,1]{2,1,0:T(8,128)} %get-tuple-element.12, f32[96,16,1022]{2,1,0:T(8,128)} %get-tuple-element.6, f32[96,16,2]{2,1,0:T(8,128)} %get-tuple-element.8, ...), kind=kLoop, calls=%fused_computation.18 | loop fusion | flops 45613056 | bytes 56624064 | tf_op jit(solution)/shard_map/convert_element_type | solution.py:80
  542.4 7.1 copy.216
  549.5 98.1 %all_to_all.102 = bf16[96,16,1024]{0,1,2:T(8,128)(2,1)} all-to-all(bf16[96,16,1024]{0,1,2:T(8,128)(2,1)} %copy.216), channel_id=1, replica_groups=mesh['gx'=8,'ao'=4] {'ao'}, dimensions={2} | all-to-all | bytes 6291456 | tf_op jit(solution)/shard_map/all_to_all | solution.py:83
  647.7 6.9 copy.217
  662.5 8.4 %fusion.5 = bf16[384,4096]{0,1:T(8,128)(2,1)} fusion(bf16[384,4096]{0,1:T(8,128)(2,1)} %copy.218, bf16[384,384]{1,0:T(8,128)(2,1)} %subtract_convert_fusion, bf16[384,4096]{1,0:T(8,128)(2,1)S(1)} %bitcast.84, bf16[384,384]{1,0:T(8,128)(2,1)S(1)} %copy-done), kind=kOutput, calls=%fused_computation.11 | convolution fusion | flops 2428502016 | bytes 10027008 | tf_op jit(solution)/shard_map/dot_general | solution.py:48
  675.0 72.5 %all_to_all.103 = bf16[384,16,256]{2,1,0:T(8,128)(2,1)S(1)} all-to-all(bf16[384,16,256]{2,1,0:T(8,128)(2,1)S(1)} %copy.220), channel_id=1, replica_groups=mesh['gx'=8,'ao'=4] {'ao'}, dimensions={0} | all-to-all | bytes 6291456 | tf_op jit(solution)/shard_map/all_to_all | solution.py:81
  (76 shorter events, 97.6 us)
Async XLA Ops:
  0.0 165.9 %copy-start = (bf16[384,384]{1,0:T(8,128)(2,1)S(1)}, bf16[384,384]{1,0:T(8,128)(2,1)}, u32[]{:S(2)}) copy-start(bf16[384,384]{1,0:T(8,128)(2,1)} %param.7) | copy-start | bytes 884740
  0.0 10.3 %copy-start.1 = (bf16[96,16,1024]{2,1,0:T(8,128)(2,1)S(1)}, bf16[96,16,1024]{2,1,0:T(8,128)(2,1)}, u32[]{:S(2)}) copy-start(bf16[96,16,1024]{2,1,0:T(8,128)(2,1)} %param.6) | copy-start | bytes 9437188
  3.6 21.9 %collective-permute-start.1 = (bf16[96,2,1024]{2,0,1:T(8,128)(2,1)}, bf16[96,2,1024]{2,0,1:T(8,128)(2,1)}, u32[]{:S(2)}, u32[]{:S(2)}) collective-permute-start(bf16[96,2,1024]{2,0,1:T(8,128)(2,1)} %copy.226), channel_id=1, source_target_pairs={{4,0},{8,4},{12,8},{16,12},{20,16},{24,20},{28,24},{0,28},{5,1},{9... | collective-permute-start | bytes 1179656 | tf_op jit(solution)/shard_map/ppermute | solution.py:20
  7.8 19.2 %collective-permute-start = (bf16[96,2,1024]{2,0,1:T(8,128)(2,1)}, bf16[96,2,1024]{2,0,1:T(8,128)(2,1)}, u32[]{:S(2)}, u32[]{:S(2)}) collective-permute-start(bf16[96,2,1024]{2,0,1:T(8,128)(2,1)} %copy.225), channel_id=1, source_target_pairs={{0,4},{4,8},{8,12},{12,16},{16,20},{20,24},{24,28},{28,0},{1,5},{5... | collective-permute-start | bytes 1179656 | tf_op jit(solution)/shard_map/ppermute | solution.py:19
  27.0 3.7 slice-start
  28.5 2.2 slice-start.1
  45.1 12.6 %copy-start.5 = (s32[384,6]{0,1:T(8,128)S(1)}, s32[384,6]{0,1:T(8,128)}, u32[]{:S(2)}) copy-start(s32[384,6]{0,1:T(8,128)} %param.9) | copy-start | bytes 27652
  45.1 12.6 %copy-start.6 = (s32[384,6]{0,1:T(8,128)S(1)}, s32[384,6]{0,1:T(8,128)}, u32[]{:S(2)}) copy-start(s32[384,6]{0,1:T(8,128)} %param.8) | copy-start | bytes 27652
  52.3 98.7 %all-to-all-start = ((bf16[96,16,1024]{0,1,2:T(8,128)(2,1)}), bf16[96,16,1024]{0,1,2:T(8,128)(2,1)}, u32[]{:S(2)}, u32[]{:S(2)}) async-start(bf16[96,16,1024]{0,1,2:T(8,128)(2,1)} %copy.196), calls=%async_computation | async-start | bytes 8388608 | tf_op jit(solution)/shard_map/all_to_all | solution.py:83
  161.1 4.8 copy-start.3
  263.6 11.4 %collective-permute-start.3 = (bf16[96,2,1024]{2,0,1:T(8,128)(2,1)S(1)}, bf16[96,2,1024]{2,0,1:T(8,128)(2,1)S(1)}, u32[]{:S(2)}, u32[]{:S(2)}) collective-permute-start(bf16[96,2,1024]{2,0,1:T(8,128)(2,1)S(1)} %copy.203), channel_id=1, source_target_pairs={{4,0},{8,4},{12,8},{16,12},{20,16},{24,20},{28,24},{0,28},{5,1},{9... | collective-permute-start | bytes 1179656 | tf_op jit(solution)/shard_map/ppermute | solution.py:20
  266.3 10.5 %collective-permute-start.2 = (bf16[96,2,1024]{2,0,1:T(8,128)(2,1)S(1)}, bf16[96,2,1024]{2,0,1:T(8,128)(2,1)S(1)}, u32[]{:S(2)}, u32[]{:S(2)}) collective-permute-start(bf16[96,2,1024]{2,0,1:T(8,128)(2,1)S(1)} %copy.202), channel_id=1, source_target_pairs={{0,4},{4,8},{8,12},{12,16},{16,20},{20,24},{24,28},{28,0},{1,5},{5... | collective-permute-start | bytes 1179656 | tf_op jit(solution)/shard_map/ppermute | solution.py:19
  407.9 4.8 copy-start.4
  510.1 12.4 %collective-permute-start.5 = (bf16[96,2,1024]{2,0,1:T(8,128)(2,1)S(1)}, bf16[96,2,1024]{2,0,1:T(8,128)(2,1)S(1)}, u32[]{:S(2)}, u32[]{:S(2)}) collective-permute-start(bf16[96,2,1024]{2,0,1:T(8,128)(2,1)S(1)} %copy.213), channel_id=1, source_target_pairs={{4,0},{8,4},{12,8},{16,12},{20,16},{24,20},{28,24},{0,28},{5,1},{9... | collective-permute-start | bytes 1179656 | tf_op jit(solution)/shard_map/ppermute | solution.py:20
  513.6 11.7 %collective-permute-start.4 = (bf16[96,2,1024]{2,0,1:T(8,128)(2,1)S(1)}, bf16[96,2,1024]{2,0,1:T(8,128)(2,1)S(1)}, u32[]{:S(2)}, u32[]{:S(2)}) collective-permute-start(bf16[96,2,1024]{2,0,1:T(8,128)(2,1)S(1)} %copy.212), channel_id=1, source_target_pairs={{0,4},{4,8},{8,12},{12,16},{16,20},{20,24},{24,28},{28,0},{1,5},{5... | collective-permute-start | bytes 1179656 | tf_op jit(solution)/shard_map/ppermute | solution.py:19
  657.7 4.8 copy-start.2
where the time goes:
time: 760 us; the launch traced here: 750 us
  blocking collectives  413 us (54%)
  local copies, waits for them, and re-layouts  138 us (18%)
  waiting for transfers between devices  107 us (14%)
  other arithmetic  51.6 us (7%)
  matrix products  25.2 us (3%)
  starting transfers between devices  15 us (2%)
    all_to_all x3, blocking collectives, per_device(): lax.all_to_all(rotate_block(lax.all_to_all(advected, 'ao', split_axis=2,...  218 us
    all_to_all x2, blocking collectives, per_device(): lax.all_to_all(advected, 'ao', split_axis=2, concat_axis=0, tiled=True)  195 us
    all_to_all x1, waiting for transfers between devices, per_device(): lax.all_to_all(advected, 'ao', split_axis=2, concat_axis=0, tiled=True)  91.6 us
    convert_element_type x3, other arithmetic, per_device(): advected = (centre - along_rows - along_columns).astype(jnp.bfloat16)  43.3 us
    dot_general x3, matrix products, rotate_block(): turned = jnp.dot(turn_matrix, drifted, preferred_element_type=jnp.float32)  25.2 us
    slice x6, local copies, waits for them, and re-layouts, per_device(): jnp.roll(centre, -2, 2)  22.7 us
    convert_element_type x3, local copies, waits for them, and re-layouts, per_device(): advected = (centre - along_rows - along_columns).astype(jnp.bfloat16)  21.5 us
    slice x6, local copies, waits for them, and re-layouts, per_device(): jnp.roll(centre, -1, 2)  21.3 us
  transfers between devices with their start and end apart: 7, of which 5 were waited for; matrix products, arithmetic and copies ran while one was open for 4% of the time, Pallas kernels for 0%

commit v1 on v0

--- a/solution.py
+++ b/solution.py
@@ -1,6 +1,10 @@
+import functools
+
 import jax
 import jax.numpy as jnp
 from jax import lax
+from jax.experimental import pallas as pl
+from jax.experimental.pallas import tpu as pltpu
 from jax.sharding import PartitionSpec as P
 
 TIME_STEPS = 3
@@ -92,9 +96,287 @@
     return current
 
 
+LANES = 128
+REACH = 2 * TIME_STEPS
+GROUP = 8
+SLOT = LANES // GROUP
+
+
+def pack_kernel(place, main_ref, before_ref, after_ref, out_ref, main, sides):
+    orients, rows, _ = main_ref.shape
+    lane = lax.broadcasted_iota(jnp.int32, (orients, LANES), 1)
+    main[...] = main_ref[...].astype(jnp.float32).reshape(orients * rows, LANES)
+    wide_lane = lax.broadcasted_iota(jnp.int32, (orients * rows, LANES), 1)
+    sides[...] = jnp.where(
+        wide_lane < LANES // 2,
+        after_ref[...].astype(jnp.float32).reshape(orients * rows, LANES),
+        before_ref[...].astype(jnp.float32).reshape(orients * rows, LANES),
+    )
+    owner = ((lane + SLOT // 2) % LANES) // SLOT
+    for group in range(rows // GROUP):
+        packed = jnp.zeros((orients, LANES), jnp.float32)
+        for slot in range(GROUP):
+            row = group * GROUP + slot
+            out_ref[1 + row] = main[pl.ds(row, orients, stride=rows), :].astype(jnp.bfloat16)
+            edge = pltpu.roll(sides[pl.ds(row, orients, stride=rows), :], SLOT * slot, 1)
+            packed = jnp.where(owner == slot, edge, packed)
+        out_ref[0 if group == 0 else rows + 1] = packed.astype(jnp.bfloat16)
+
+
+def pack(density, place, shift, part, devices, parts):
+    share, rows, columns = density.shape
+    tiles = columns // LANES
+    step = 32
+
+    def tile(offset):
+        def index(block, place_ref):
+            target = lax.rem(place_ref[0] + shift, devices)
+            return block, 0, lax.rem(target * parts + part + offset + tiles, tiles)
+
+        return pl.BlockSpec((step, rows, LANES), index)
+
+    return pl.pallas_call(
+        pack_kernel,
+        grid_spec=pltpu.PrefetchScalarGridSpec(
+            num_scalar_prefetch=1,
+            grid=(share // step,),
+            in_specs=[tile(0), tile(-1), tile(1)],
+            out_specs=pl.BlockSpec((rows + 2, step, LANES), lambda block, place_ref: (0, block, 0)),
+            scratch_shapes=[pltpu.VMEM((step * rows, LANES), jnp.float32)] * 2,
+        ),
+        out_shape=jax.ShapeDtypeStruct((rows + 2, share, LANES), jnp.bfloat16),
+        name="pack",
+    )(place, density, density, density)
+
+
+def unpack_kernel(devices, place, *refs):
+    blocks, out_ref, wide = refs[:devices], refs[-2], refs[-1]
+    rows, share, _ = blocks[0].shape
+    for shift in range(devices):
+
+        @pl.when(pl.program_id(0) == shift)
+        def _():
+            wide[...] = blocks[shift][...].astype(jnp.float32).reshape(rows * share, LANES)
+            for orient in range(share):
+                out_ref[orient] = wide[pl.ds(orient, rows, stride=share), :].astype(jnp.bfloat16)
+
+
+def unpack(blocks, place, part, parts, shape, before):
+    devices = len(blocks)
+    rows, share, _ = blocks[0].shape
+
+    def index(shift, place_ref):
+        return 0, 0, lax.rem(place_ref[0] + shift, devices) * parts + part
+
+    whole = pl.BlockSpec(blocks[0].shape, lambda shift, place_ref: (0, 0, 0))
+    earlier = () if before is None else (before,)
+    return pl.pallas_call(
+        functools.partial(unpack_kernel, devices),
+        grid_spec=pltpu.PrefetchScalarGridSpec(
+            num_scalar_prefetch=1,
+            grid=(devices,),
+            in_specs=[whole] * devices + [pl.BlockSpec(memory_space=pl.ANY)] * len(earlier),
+            out_specs=pl.BlockSpec((share, rows, LANES), index),
+            scratch_shapes=[pltpu.VMEM((rows * share, LANES), jnp.float32)],
+        ),
+        out_shape=jax.ShapeDtypeStruct(shape, jnp.bfloat16),
+        input_output_aliases={1 + devices: 0} if earlier else {},
+        name="unpack",
+    )(place, *blocks, *earlier)
+
+
+def steps_kernel(devices, *refs):
+    blocks = refs[:devices]
+    above, below, kernel, turn, keep, by_row, by_column, choose = refs[devices : devices + 8]
+    outs = refs[devices + 8 : 2 * devices + 8]
+    first, second, advected = refs[2 * devices + 8 :]
+    share = blocks[0].shape[1]
+    number = share * devices
+    rows = outs[0].shape[0]
+
+    def turned_back(value, slot):
+        return pltpu.roll(value.astype(jnp.float32), (LANES - SLOT * slot) % LANES, 1).astype(jnp.bfloat16)
+
+    for index in range(rows + 2 * REACH):
+        row = index - REACH
+        slot = row % GROUP
+        if row < 0:
+            first[index, :, :LANES] = above[index]
+            first[index, :, LANES:] = turned_back(above[REACH], slot)
+        elif row >= rows:
+            first[index, :, :LANES] = below[1 + row - rows]
+            first[index, :, LANES:] = turned_back(below[0], slot)
+        else:
+            for part in range(devices):
+                span = slice(part * share, (part + 1) * share)
+                first[index, span, :LANES] = blocks[part][1 + row]
+                first[index, span, LANES:] = turned_back(blocks[part][0 if row < GROUP else rows + 1], slot)
+
+    block = 48
+
+    def advect(source, row, tiles, target, column):
+        lane = lax.broadcasted_iota(jnp.int32, (block, LANES), 1)
+        for start in range(0, number, block):
+            span = slice(start, start + block)
+            forward_row = choose[0, span] > 0
+            forward_column = choose[1, span] > 0
+            depth = jnp.where(forward_column, lane, LANES - 1 - lane)
+            edge_one, edge_two = depth < 1, depth < 2
+            centres, ones, twos = [], [], []
+            for tile in range(2):
+                centre = source[row + 2, span, tile * LANES : (tile + 1) * LANES].astype(jnp.float32)
+                centres.append(centre)
+                ones.append(jnp.where(forward_column, pltpu.roll(centre, 1, 1), pltpu.roll(centre, LANES - 1, 1)))
+                twos.append(jnp.where(forward_column, pltpu.roll(centre, 2, 1), pltpu.roll(centre, LANES - 2, 1)))
+            for tile in range(tiles):
+                lanes = slice(tile * LANES, (tile + 1) * LANES)
+
+                def at(offset):
+                    return source[row + 2 + offset, span, lanes].astype(jnp.float32)
+
+                row_one = jnp.where(forward_row, at(-1), at(1))
+                row_two = jnp.where(forward_row, at(-2), at(2))
+                column_one = jnp.where(edge_one, ones[1 - tile], ones[tile])
+                column_two = jnp.where(edge_two, twos[1 - tile], twos[tile])
+                value = (
+                    keep[span] * centres[tile]
+                    + by_row[span] * (row_one - 0.25 * row_two)
+                    + by_column[span] * (column_one - 0.25 * column_two)
+                )
+                target[span, column + tile * LANES : column + (tile + 1) * LANES] = value.astype(jnp.bfloat16)
+
+    def rotate(values):
+        potential = jnp.dot(kernel[...], values[...], preferred_element_type=jnp.float32)
+        drifted = (values[...].astype(jnp.float32) * (1.0 + potential)).astype(jnp.bfloat16)
+        turned = jnp.dot(turn[...], drifted, preferred_element_type=jnp.float32)
+        return (values[...].astype(jnp.float32) + rotation_rate * turned).astype(jnp.bfloat16)
+
+    buffers = [first, second]
+    for step in range(TIME_STEPS - 1):
+        source, target = buffers[step % 2], buffers[(step + 1) % 2]
+
+        @pl.loop(0, (rows + 2 * REACH - 4 * (step + 1)) // 2)
+        def _(pair):
+            row = 2 * pair
+            for half in range(2):
+                advect(source, row + half, 2, advected.at[half], 0)
+            for half in range(2):
+                target[row + half] = rotate(advected.at[half])
+
+    source = buffers[(TIME_STEPS - 1) % 2]
+
+    @pl.loop(0, rows // 4)
+    def _(quad):
+        row = 4 * quad
+        for half in range(2):
+            for side in range(2):
+                advect(source, row + 2 * half + side, 1, advected.at[half], side * LANES)
+        for half in range(2):
+            result = rotate(advected.at[half])
+            for side in range(2):
+                for part in range(devices):
+                    outs[part][row + 2 * half + side] = result[
+                        part * share : (part + 1) * share, side * LANES : (side + 1) * LANES
+                    ]
+
+
+def three_steps(blocks, above, below, kernel, turn, coefficients):
+    devices = len(blocks)
+    rows, share, _ = blocks[0].shape
+    rows -= 2
+    number = share * devices
+    cells = (rows + 2 * REACH) * 2 * LANES
+    vmem = pl.BlockSpec(memory_space=pltpu.VMEM)
+    operands = (*blocks, above, below, kernel, turn, *coefficients)
+    return pl.pallas_call(
+        functools.partial(steps_kernel, devices),
+        in_specs=[vmem] * len(operands),
+        out_specs=[vmem] * devices,
+        out_shape=[jax.ShapeDtypeStruct((rows, share, LANES), jnp.bfloat16)] * devices,
+        scratch_shapes=[
+            pltpu.VMEM((rows + 2 * REACH, number, 2 * LANES), jnp.bfloat16),
+            pltpu.VMEM((rows + 2 * REACH - 4, number, 2 * LANES), jnp.bfloat16),
+            pltpu.VMEM((2, number, 2 * LANES), jnp.bfloat16),
+        ],
+        compiler_params=pltpu.CompilerParams(vmem_limit_bytes=48 * 2**20),
+        cost_estimate=pl.CostEstimate(
+            flops=12 * number * number * cells, bytes_accessed=8 * 2**20, transcendentals=0
+        ),
+        name="three_steps",
+    )(*operands)
+
+
+def blocked(density, kernel, neighbours, weights, signs, speeds):
+    devices = lax.axis_size("ao")
+    share, rows, columns = density.shape
+    parts = columns // devices // LANES
+    here = lax.axis_index("ao")
+    place = here.astype(jnp.int32).reshape(1)
+
+    packed = [[pack(density, place, shift, part, devices, parts) for shift in range(devices)] for part in range(parts)]
+
+    def turned(value, dim):
+        pieces = [
+            lax.dynamic_slice_in_dim(value, lax.rem(here - shift + devices, devices) * share, share, dim)
+            for shift in range(devices)
+        ]
+        return jnp.concatenate(pieces, dim)
+
+    turn = turned(turned(stencil_matrix(neighbours, weights), 0), 1)
+    kernel = turned(turned(kernel, 0), 1)
+    signs, speeds = turned(signs, 1), turned(speeds, 1)
+
+    def spread(value):
+        return jnp.broadcast_to(value[..., None], value.shape + (LANES,))
+
+    coefficients = (
+        spread(1.0 - 1.5 * (speeds[0] + speeds[1])),
+        spread(2.0 * speeds[0]),
+        spread(2.0 * speeds[1]),
+        spread((signs == 1).astype(jnp.float32)),
+    )
+
+    size = lax.axis_size("gx")
+    up = [(i, (i + 1) % size) for i in range(size)]
+    down = [(j, i) for i, j in up]
+    evolved = None
+    arrived = None
+    results = []
+    for part in range(parts):
+        blocks = packed[part]
+        if arrived is not None:
+            blocks, _ = lax.optimization_barrier((blocks, arrived))
+        arrived = [blocks[0]] + [
+            lax.ppermute(blocks[shift], "ao", [(i, (i + shift) % devices) for i in range(devices)])
+            for shift in range(1, devices)
+        ]
+        above = lax.ppermute(jnp.concatenate([block[-(REACH + 1) :] for block in arrived], 1), "gx", up)
+        below = lax.ppermute(jnp.concatenate([block[: REACH + 1] for block in arrived], 1), "gx", down)
+        results.append(three_steps(arrived, above, below, kernel, turn, coefficients))
+    for part in range(parts):
+        result = results[part]
+        returned = [result[0]] + [
+            lax.ppermute(result[shift], "ao", [(i, (i - shift) % devices) for i in range(devices)])
+            for shift in range(1, devices)
+        ]
+        evolved = unpack(returned, place, part, parts, density.shape, evolved)
+    return evolved
+
+
 def solution(mesh):
     in_specs = (P("ao", "gx", None), P(), P(), P(), P(), P())
     out_specs = P("ao", "gx", None)
-    return jax.shard_map(
-        per_device, mesh=mesh, in_specs=in_specs, out_specs=out_specs, check_vma=False
-    )
+
+    def run(density, *rest):
+        share, rows, columns = (
+            density.shape[0] // mesh.shape["ao"],
+            density.shape[1] // mesh.shape["gx"],
+            density.shape[2] // mesh.shape["ao"],
+        )
+        fits = columns % LANES == 0 and share % 32 == 0 and rows == 2 * GROUP
+        body = jax.shard_map(
+            blocked if fits else per_device, mesh=mesh, in_specs=in_specs, out_specs=out_specs, check_vma=False
+        )
+        return body(density, *rest)
+
+    return run

time: 760 us -> 214 us (0.28); the launches traced: 750 us -> 214 us
  blocking collectives: 413 us -> 0 us
  local copies, waits for them, and re-layouts: 138 us -> 6.02 us
  Pallas kernels: 0 us -> 111 us
  waiting for transfers between devices: 107 us -> 53.2 us
  other arithmetic: 51.6 us -> 1.81 us
  starting transfers between devices: 15 us -> 41.5 us
  matrix products: 25.2 us -> 0 us
    all_to_all x5 -> x0, blocking collectives: 413 us -> none  [the longest x3 218 us: per_device(): lax.all_to_all(rotate_block(lax.all_to_all(advected, 'ao', split_axis=2,...]
    pallas_call x0 -> x12, Pallas kernels: none -> 111 us  [the longest x2 76 us: three_steps(): pl.pallas_call(functools.partial(steps_kernel, devices), in_specs=[vmem]...]
    all_to_all x1 -> x0, waiting for transfers between devices: 91.6 us -> none  [per_device(): lax.all_to_all(advected, 'ao', split_axis=2, concat_axis=0, tiled=True)]
    convert_element_type x6 -> x1, other arithmetic: 49.9 us -> 0.08 us  [blocked(): (signs == 1).astype(jnp.float32)]
    slice x19 -> x8, local copies, waits for them, and re-layouts: 48.5 us -> 0.19 us  [blocked(): block[:REACH + 1]]
    ppermute x6 -> x16, waiting for transfers between devices: 15.8 us -> 53.2 us  [the longest x6 27.1 us: blocked(): lax.ppermute(result[shift], 'ao', [(i, (i - shift) % devices) for i in ra...]
    ppermute x6 -> x16, starting transfers between devices: 9.66 us -> 41.5 us  [the longest x6 19.3 us: blocked(): lax.ppermute(blocks[shift], 'ao', [(i, (i + shift) % devices) for i in ra...]
    reshape x6 -> x0, local copies, waits for them, and re-layouts: 26.7 us -> none  [the longest x3 14.4 us: rotate_block(): values = block.reshape(block_shape[0], -1)]
  transfers between devices with their start and end apart: 7 -> 16, of which waited for: 5 -> 5; matrix products, arithmetic and copies ran while one was open for 4% -> 1% of each run, Pallas kernels for 0% -> 48%
where the time goes in v1:
time: 214 us
  Pallas kernels  111 us (52%)
  waiting for transfers between devices  53.2 us (25%)
  starting transfers between devices  41.5 us (19%)
  local copies, waits for them, and re-layouts  6.02 us (3%)
    pallas_call x2, Pallas kernels, three_steps(): pl.pallas_call(functools.partial(steps_kernel, devices), in_specs=[vmem]...  76 us
    ppermute x6, waiting for transfers between devices, blocked(): lax.ppermute(result[shift], 'ao', [(i, (i - shift) % devices) for i in ra...  27.1 us
    ppermute x6, waiting for transfers between devices, blocked(): lax.ppermute(blocks[shift], 'ao', [(i, (i + shift) % devices) for i in ra...  26.1 us
    pallas_call x8, Pallas kernels, pack(): pl.pallas_call(pack_kernel, grid_spec=pltpu.PrefetchScalarGridSpec(num_sc...  26.1 us
    ppermute x6, starting transfers between devices, blocked(): lax.ppermute(blocks[shift], 'ao', [(i, (i + shift) % devices) for i in ra...  19.3 us
    ppermute x6, starting transfers between devices, blocked(): lax.ppermute(result[shift], 'ao', [(i, (i - shift) % devices) for i in ra...  16.7 us
    pallas_call x2, Pallas kernels, unpack(): pl.pallas_call(functools.partial(unpack_kernel, devices), grid_spec=pltpu...  8.69 us
    ppermute x2, starting transfers between devices, blocked(): lax.ppermute(jnp.concatenate([block[:REACH + 1] for block in arrived], 1)...  5.35 us
  transfers between devices with their start and end apart: 16, of which 5 were waited for; matrix products, arithmetic and copies ran while one was open for 1% of the time, Pallas kernels for 48%

profile of v1, /device:TPU:0, one launch (start us, length us, event | category | flops | bytes accessed | tf_op | source)
XLA Modules:
  0.0 213.6 jit_solution(1182503429092257479)
XLA Ops:
  0.0 3.3 %pack.13 = bf16[18,96,128]{2,1,0:T(8,128)(2,1)} custom-call(s32[1]{0:T(128)} %bitcast.place, bf16[96,16,1024]{2,1,0:T(8,128)(2,1)} %after_ref.15, bf16[96,16,1024]{2,1,0:T(8,128)(2,1)} %after_ref.15, bf16[96,16,1024]{2,1,0:T(8,128)(2,1)} %after_ref.15), custom_call_target="tpu_custom_call" | custom-call | tf_op jit(solution)/shard_map/pack/pallas_call | solution.py:138
  3.3 3.0 %collective-permute-start = (bf16[18,96,128]{2,1,0:T(8,128)(2,1)}, bf16[18,96,128]{2,1,0:T(8,128)(2,1)S(1)}, u32[]{:S(2)}, u32[]{:S(2)}) collective-permute-start(bf16[18,96,128]{2,1,0:T(8,128)(2,1)} %pack.13), channel_id=1, source_target_pairs={{0,1},{1,2},{2,3},{3,0},{4,5},{5,6},{6,7},{7,4},{8,9},{9,10},{10,1... | collective-permute-start | bytes 1327112 | tf_op jit(solution)/shard_map/ppermute | solution.py:350
  6.3 3.3 %pack.14 = bf16[18,96,128]{2,1,0:T(8,128)(2,1)} custom-call(s32[1]{0:T(128)} %bitcast.place, bf16[96,16,1024]{2,1,0:T(8,128)(2,1)} %after_ref.15, bf16[96,16,1024]{2,1,0:T(8,128)(2,1)} %after_ref.15, bf16[96,16,1024]{2,1,0:T(8,128)(2,1)} %after_ref.15), custom_call_target="tpu_custom_call" | custom-call | tf_op jit(solution)/shard_map/pack/pallas_call | solution.py:138
  9.6 2.6 %collective-permute-start.1 = (bf16[18,96,128]{2,1,0:T(8,128)(2,1)}, bf16[18,96,128]{2,1,0:T(8,128)(2,1)S(1)}, u32[]{:S(2)}, u32[]{:S(2)}) collective-permute-start(bf16[18,96,128]{2,1,0:T(8,128)(2,1)} %pack.14), channel_id=1, source_target_pairs={{0,2},{1,3},{2,0},{3,1},{4,6},{5,7},{6,4},{7,5},{8,10},{9,11},{10,... | collective-permute-start | bytes 1327112 | tf_op jit(solution)/shard_map/ppermute | solution.py:350
  12.1 3.3 %pack.15 = bf16[18,96,128]{2,1,0:T(8,128)(2,1)} custom-call(s32[1]{0:T(128)} %bitcast.place, bf16[96,16,1024]{2,1,0:T(8,128)(2,1)} %after_ref.15, bf16[96,16,1024]{2,1,0:T(8,128)(2,1)} %after_ref.15, bf16[96,16,1024]{2,1,0:T(8,128)(2,1)} %after_ref.15), custom_call_target="tpu_custom_call" | custom-call | tf_op jit(solution)/shard_map/pack/pallas_call | solution.py:138
  16.8 3.2 %pack.8.refs_0_ = bf16[18,96,128]{2,1,0:T(8,128)(2,1)} custom-call(s32[1]{0:T(128)} %bitcast.place, bf16[96,16,1024]{2,1,0:T(8,128)(2,1)} %after_ref.15, bf16[96,16,1024]{2,1,0:T(8,128)(2,1)} %after_ref.15, bf16[96,16,1024]{2,1,0:T(8,128)(2,1)} %after_ref.15), custom_call_target="tpu_custom_call" | custom-call | tf_op jit(solution)/shard_map/pack/pallas_call | solution.py:138
  20.0 3.3 %pack.9 = bf16[18,96,128]{2,1,0:T(8,128)(2,1)} custom-call(s32[1]{0:T(128)} %bitcast.place, bf16[96,16,1024]{2,1,0:T(8,128)(2,1)} %after_ref.15, bf16[96,16,1024]{2,1,0:T(8,128)(2,1)} %after_ref.15, bf16[96,16,1024]{2,1,0:T(8,128)(2,1)} %after_ref.15), custom_call_target="tpu_custom_call" | custom-call | tf_op jit(solution)/shard_map/pack/pallas_call | solution.py:138
  23.3 3.2 %pack.10 = bf16[18,96,128]{2,1,0:T(8,128)(2,1)} custom-call(s32[1]{0:T(128)} %bitcast.place, bf16[96,16,1024]{2,1,0:T(8,128)(2,1)} %after_ref.15, bf16[96,16,1024]{2,1,0:T(8,128)(2,1)} %after_ref.15, bf16[96,16,1024]{2,1,0:T(8,128)(2,1)} %after_ref.15), custom_call_target="tpu_custom_call" | custom-call | tf_op jit(solution)/shard_map/pack/pallas_call | solution.py:138
  26.5 3.2 %pack.11 = bf16[18,96,128]{2,1,0:T(8,128)(2,1)} custom-call(s32[1]{0:T(128)} %bitcast.place, bf16[96,16,1024]{2,1,0:T(8,128)(2,1)} %after_ref.15, bf16[96,16,1024]{2,1,0:T(8,128)(2,1)} %after_ref.15, bf16[96,16,1024]{2,1,0:T(8,128)(2,1)} %after_ref.15), custom_call_target="tpu_custom_call" | custom-call | tf_op jit(solution)/shard_map/pack/pallas_call | solution.py:138
  29.8 3.3 %pack.12.refs_0_ = bf16[18,96,128]{2,1,0:T(8,128)(2,1)} custom-call(s32[1]{0:T(128)} %bitcast.place, bf16[96,16,1024]{2,1,0:T(8,128)(2,1)} %after_ref.15, bf16[96,16,1024]{2,1,0:T(8,128)(2,1)} %after_ref.15, bf16[96,16,1024]{2,1,0:T(8,128)(2,1)} %after_ref.15), custom_call_target="tpu_custom_call" | custom-call | tf_op jit(solution)/shard_map/pack/pallas_call | solution.py:138
  35.7 2.1 collective-permute-done.1.refs_2_
  37.8 9.9 %collective-permute-start.3 = (bf16[18,96,128]{2,1,0:T(8,128)(2,1)S(1)}, bf16[18,96,128]{2,1,0:T(8,128)(2,1)S(1)}, u32[]{:S(2)}, u32[]{:S(2)}) collective-permute-start(bf16[18,96,128]{2,1,0:T(8,128)(2,1)S(1)} %copy-done.4), channel_id=1, source_target_pairs={{0,1},{1,2},{2,3},{3,0},{4,5},{5,6},{6,7},{7,4},{8,9},{9,10},{10,1... | collective-permute-start | bytes 1327112 | tf_op jit(solution)/shard_map/ppermute | solution.py:350
  47.7 1.6 collective-permute-start.4
  50.4 2.7 %collective-permute-start.12 = (bf16[7,384,128]{2,1,0:T(8,128)(2,1)S(1)}, bf16[7,384,128]{2,1,0:T(8,128)(2,1)S(1)}, u32[]{:S(2)}, u32[]{:S(2)}) collective-permute-start(bf16[7,384,128]{2,1,0:T(8,128)(2,1)S(1)} %pad_maximum_fusion.3), channel_id=1, source_target_pairs={{4,0},{8,4},{12,8},{16,12},{20,16},{24,20},{28,24},{0,28},{5,1},{9... | collective-permute-start | bytes 2064392 | tf_op jit(solution)/shard_map/ppermute | solution.py:354
  53.1 23.2 %collective-permute-done.5.refs_3_ = bf16[18,96,128]{2,1,0:T(8,128)(2,1)S(1)} collective-permute-done((bf16[18,96,128]{2,1,0:T(8,128)(2,1)S(1)}, bf16[18,96,128]{2,1,0:T(8,128)(2,1)S(1)}, u32[]{:S(2)}, u32[]{:S(2)}) %collective-permute-start.5) | collective-permute-done | bytes 442400 | tf_op jit(solution)/shard_map/ppermute | solution.py:350
  77.4 2.7 %collective-permute-start.7 = (bf16[7,384,128]{2,1,0:T(8,128)(2,1)S(1)}, bf16[7,384,128]{2,1,0:T(8,128)(2,1)S(1)}, u32[]{:S(2)}, u32[]{:S(2)}) collective-permute-start(bf16[7,384,128]{2,1,0:T(8,128)(2,1)S(1)} %pad_maximum_fusion.1), channel_id=1, source_target_pairs={{4,0},{8,4},{12,8},{16,12},{20,16},{24,20},{28,24},{0,28},{5,1},{9... | collective-permute-start | bytes 2064392 | tf_op jit(solution)/shard_map/ppermute | solution.py:354
  80.9 38.0 %three_steps.3 = (bf16[16,96,128]{2,1,0:T(8,128)(2,1)S(1)}, bf16[16,96,128]{2,1,0:T(8,128)(2,1)S(1)}, bf16[16,96,128]{2,1,0:T(8,128)(2,1)S(1)}, bf16[16,96,128]{2,1,0:T(8,128)(2,1)S(1)}) custom-call(bf16[18,96,128]{2,1,0:T(8,128)(2,1)S(1)} %copy-done.1, bf16[18,96,128]{2,1,0:T(8,128)(2,1)S(1)} %collective-permute-done.refs_1_, ...), custom_call_target="tpu_custom_call" | custom-call | flops 12683575296 | bytes 8388608 | tf_op jit(solution)/shard_map/three_steps/pallas_call | solution.py:291
  119.7 11.7 %collective-permute-start.13 = (bf16[16,96,128]{2,1,0:T(8,128)(2,1)S(1)}, bf16[16,96,128]{2,1,0:T(8,128)(2,1)S(1)}, u32[]{:S(2)}, u32[]{:S(2)}) collective-permute-start(bf16[16,96,128]{2,1,0:T(8,128)(2,1)S(1)} %get-tuple-element.26), channel_id=1, source_target_pairs={{0,3},{1,0},{2,1},{3,2},{4,7},{5,4},{6,5},{7,6},{8,11},{9,8},{10,9... | collective-permute-start | bytes 1179656 | tf_op jit(solution)/shard_map/ppermute | solution.py:359
  132.8 38.0 %three_steps.2 = (bf16[16,96,128]{2,1,0:T(8,128)(2,1)S(1)}, bf16[16,96,128]{2,1,0:T(8,128)(2,1)S(1)}, bf16[16,96,128]{2,1,0:T(8,128)(2,1)S(1)}, bf16[16,96,128]{2,1,0:T(8,128)(2,1)S(1)}) custom-call(bf16[18,96,128]{2,1,0:T(8,128)(2,1)S(1)} %copy-done, bf16[18,96,128]{2,1,0:T(8,128)(2,1)S(1)} %collective-permute-done.3.refs_1_, ...), custom_call_target="tpu_custom_call" | custom-call | flops 12683575296 | bytes 8388608 | tf_op jit(solution)/shard_map/three_steps/pallas_call | solution.py:291
  171.5 3.3 %collective-permute-start.8 = (bf16[16,96,128]{2,1,0:T(8,128)(2,1)S(1)}, bf16[16,96,128]{2,1,0:T(8,128)(2,1)S(1)}, u32[]{:S(2)}, u32[]{:S(2)}) collective-permute-start(bf16[16,96,128]{2,1,0:T(8,128)(2,1)S(1)} %get-tuple-element.22), channel_id=1, source_target_pairs={{0,3},{1,0},{2,1},{3,2},{4,7},{5,4},{6,5},{7,6},{8,11},{9,8},{10,9... | collective-permute-start | bytes 1179656 | tf_op jit(solution)/shard_map/ppermute | solution.py:359
  176.9 4.3 %unpack.2.refs_4_ = bf16[96,16,1024]{2,1,0:T(8,128)(2,1)} custom-call(s32[1]{0:T(128)} %bitcast.place, bf16[16,96,128]{2,1,0:T(8,128)(2,1)} %copy-done.3, bf16[16,96,128]{2,1,0:T(8,128)(2,1)} %copy-done.10, bf16[16,96,128]{2,1,0:T(8,128)(2,1)} %copy-done.11, bf16[16,96,128]{2,1,0:T(8,128)(2,1)} %copy-done.12), custom_call_target="tpu_custom_call" | custom-call | tf_op jit(solution)/shard_map/unpack/pallas_call | solution.py:173
  181.3 3.1 %collective-permute-done.8.refs_1_ = bf16[16,96,128]{2,1,0:T(8,128)(2,1)S(1)} collective-permute-done((bf16[16,96,128]{2,1,0:T(8,128)(2,1)S(1)}, bf16[16,96,128]{2,1,0:T(8,128)(2,1)S(1)}, u32[]{:S(2)}, u32[]{:S(2)}) %collective-permute-start.8) | collective-permute-done | bytes 393248 | tf_op jit(solution)/shard_map/ppermute | solution.py:359
  184.4 23.9 %collective-permute-done.9.refs_2_ = bf16[16,96,128]{2,1,0:T(8,128)(2,1)S(1)} collective-permute-done((bf16[16,96,128]{2,1,0:T(8,128)(2,1)S(1)}, bf16[16,96,128]{2,1,0:T(8,128)(2,1)S(1)}, u32[]{:S(2)}, u32[]{:S(2)}) %collective-permute-start.9) | collective-permute-done | bytes 393248 | tf_op jit(solution)/shard_map/ppermute | solution.py:359
  209.2 4.3 %unpack.3 = bf16[96,16,1024]{2,1,0:T(8,128)(2,1)} custom-call(s32[1]{0:T(128)} %bitcast.place, bf16[16,96,128]{2,1,0:T(8,128)(2,1)} %copy-done.2, bf16[16,96,128]{2,1,0:T(8,128)(2,1)} %copy-done.7, bf16[16,96,128]{2,1,0:T(8,128)(2,1)} %copy-done.8, bf16[16,96,128]{2,1,0:T(8,128)(2,1)} %copy-done.9, ...), custom_call_target="tpu_custom_call", output_to_operand_aliasing={{}: (5, {})} | custom-call | tf_op jit(solution)/shard_map/unpack/pallas_call | solution.py:173
  (92 shorter events, 12.6 us)
Async XLA Ops:
  3.3 32.4 %collective-permute-start = (bf16[18,96,128]{2,1,0:T(8,128)(2,1)}, bf16[18,96,128]{2,1,0:T(8,128)(2,1)S(1)}, u32[]{:S(2)}, u32[]{:S(2)}) collective-permute-start(bf16[18,96,128]{2,1,0:T(8,128)(2,1)} %pack.13), channel_id=1, source_target_pairs={{0,1},{1,2},{2,3},{3,0},{4,5},{5,6},{6,7},{7,4},{8,9},{9,10},{10,1... | collective-permute-start | bytes 1327112 | tf_op jit(solution)/shard_map/ppermute | solution.py:350
  9.6 28.2 %collective-permute-start.1 = (bf16[18,96,128]{2,1,0:T(8,128)(2,1)}, bf16[18,96,128]{2,1,0:T(8,128)(2,1)S(1)}, u32[]{:S(2)}, u32[]{:S(2)}) collective-permute-start(bf16[18,96,128]{2,1,0:T(8,128)(2,1)} %pack.14), channel_id=1, source_target_pairs={{0,2},{1,3},{2,0},{3,1},{4,6},{5,7},{6,4},{7,5},{8,10},{9,11},{10,... | collective-permute-start | bytes 1327112 | tf_op jit(solution)/shard_map/ppermute | solution.py:350
  15.4 22.3 %collective-permute-start.2 = (bf16[18,96,128]{2,1,0:T(8,128)(2,1)}, bf16[18,96,128]{2,1,0:T(8,128)(2,1)S(1)}, u32[]{:S(2)}, u32[]{:S(2)}) collective-permute-start(bf16[18,96,128]{2,1,0:T(8,128)(2,1)} %pack.15), channel_id=1, source_target_pairs={{0,3},{1,0},{2,1},{3,2},{4,7},{5,4},{6,5},{7,6},{8,11},{9,8},{10,9... | collective-permute-start | bytes 1327112 | tf_op jit(solution)/shard_map/ppermute | solution.py:350
  29.7 3.3 %copy-start.14 = (s32[384,6]{0,1:T(8,128)S(1)}, s32[384,6]{0,1:T(8,128)}, u32[]{:S(2)}) copy-start(s32[384,6]{0,1:T(8,128)} %param.9) | copy-start | bytes 27652
  29.7 3.4 %copy-start.15 = (s32[384,6]{0,1:T(8,128)S(1)}, s32[384,6]{0,1:T(8,128)}, u32[]{:S(2)}) copy-start(s32[384,6]{0,1:T(8,128)} %param.8) | copy-start | bytes 27652
  33.1 1.3 copy-start.17
  35.0 2.8 %copy-start.4 = (bf16[18,96,128]{2,1,0:T(8,128)(2,1)S(1)}, bf16[18,96,128]{2,1,0:T(8,128)(2,1)}, u32[]{:S(2)}) copy-start(bf16[18,96,128]{2,1,0:T(8,128)(2,1)} %pack.9) | copy-start | bytes 1327108
  35.0 12.7 %copy-start.5 = (bf16[18,96,128]{2,1,0:T(8,128)(2,1)S(1)}, bf16[18,96,128]{2,1,0:T(8,128)(2,1)}, u32[]{:S(2)}) copy-start(bf16[18,96,128]{2,1,0:T(8,128)(2,1)} %pack.10) | copy-start | bytes 1327108
  35.0 14.4 %copy-start.6 = (bf16[18,96,128]{2,1,0:T(8,128)(2,1)S(1)}, bf16[18,96,128]{2,1,0:T(8,128)(2,1)}, u32[]{:S(2)}) copy-start(bf16[18,96,128]{2,1,0:T(8,128)(2,1)} %pack.11) | copy-start | bytes 1327108
  37.8 39.4 %collective-permute-start.3 = (bf16[18,96,128]{2,1,0:T(8,128)(2,1)S(1)}, bf16[18,96,128]{2,1,0:T(8,128)(2,1)S(1)}, u32[]{:S(2)}, u32[]{:S(2)}) collective-permute-start(bf16[18,96,128]{2,1,0:T(8,128)(2,1)S(1)} %copy-done.4), channel_id=1, source_target_pairs={{0,1},{1,2},{2,3},{3,0},{4,5},{5,6},{6,7},{7,4},{8,9},{9,10},{10,1... | collective-permute-start | bytes 1327112 | tf_op jit(solution)/shard_map/ppermute | solution.py:350
  47.7 29.5 %collective-permute-start.4 = (bf16[18,96,128]{2,1,0:T(8,128)(2,1)S(1)}, bf16[18,96,128]{2,1,0:T(8,128)(2,1)S(1)}, u32[]{:S(2)}, u32[]{:S(2)}) collective-permute-start(bf16[18,96,128]{2,1,0:T(8,128)(2,1)S(1)} %copy-done.5), channel_id=1, source_target_pairs={{0,2},{1,3},{2,0},{3,1},{4,6},{5,7},{6,4},{7,5},{8,10},{9,11},{10,... | collective-permute-start | bytes 1327112 | tf_op jit(solution)/shard_map/ppermute | solution.py:350
  49.3 27.0 %collective-permute-start.5 = (bf16[18,96,128]{2,1,0:T(8,128)(2,1)S(1)}, bf16[18,96,128]{2,1,0:T(8,128)(2,1)S(1)}, u32[]{:S(2)}, u32[]{:S(2)}) collective-permute-start(bf16[18,96,128]{2,1,0:T(8,128)(2,1)S(1)} %copy-done.6), channel_id=1, source_target_pairs={{0,3},{1,0},{2,1},{3,2},{4,7},{5,4},{6,5},{7,6},{8,11},{9,8},{10,9... | collective-permute-start | bytes 1327112 | tf_op jit(solution)/shard_map/ppermute | solution.py:350
  50.2 2.9 %copy-start = (bf16[18,96,128]{2,1,0:T(8,128)(2,1)S(1)}, bf16[18,96,128]{2,1,0:T(8,128)(2,1)}, u32[]{:S(2)}) copy-start(bf16[18,96,128]{2,1,0:T(8,128)(2,1)} %pack.8.refs_0_) | copy-start | bytes 1327108
  50.3 29.8 %collective-permute-start.11 = (bf16[7,384,128]{2,1,0:T(8,128)(2,1)S(1)}, bf16[7,384,128]{2,1,0:T(8,128)(2,1)S(1)}, u32[]{:S(2)}, u32[]{:S(2)}) collective-permute-start(bf16[7,384,128]{2,1,0:T(8,128)(2,1)S(1)} %pad_maximum_fusion.2), channel_id=1, source_target_pairs={{0,4},{4,8},{8,12},{12,16},{16,20},{20,24},{24,28},{28,0},{1,5},{5... | collective-permute-start | bytes 2064392 | tf_op jit(solution)/shard_map/ppermute | solution.py:353
  50.4 29.7 %collective-permute-start.12 = (bf16[7,384,128]{2,1,0:T(8,128)(2,1)S(1)}, bf16[7,384,128]{2,1,0:T(8,128)(2,1)S(1)}, u32[]{:S(2)}, u32[]{:S(2)}) collective-permute-start(bf16[7,384,128]{2,1,0:T(8,128)(2,1)S(1)} %pad_maximum_fusion.3), channel_id=1, source_target_pairs={{4,0},{8,4},{12,8},{16,12},{20,16},{24,20},{28,24},{0,28},{5,1},{9... | collective-permute-start | bytes 2064392 | tf_op jit(solution)/shard_map/ppermute | solution.py:354
  77.3 54.7 %collective-permute-start.6 = (bf16[7,384,128]{2,1,0:T(8,128)(2,1)S(1)}, bf16[7,384,128]{2,1,0:T(8,128)(2,1)S(1)}, u32[]{:S(2)}, u32[]{:S(2)}) collective-permute-start(bf16[7,384,128]{2,1,0:T(8,128)(2,1)S(1)} %pad_maximum_fusion), channel_id=1, source_target_pairs={{0,4},{4,8},{8,12},{12,16},{16,20},{20,24},{24,28},{28,0},{1,5},{5... | collective-permute-start | bytes 2064392 | tf_op jit(solution)/shard_map/ppermute | solution.py:353
  77.4 54.5 %collective-permute-start.7 = (bf16[7,384,128]{2,1,0:T(8,128)(2,1)S(1)}, bf16[7,384,128]{2,1,0:T(8,128)(2,1)S(1)}, u32[]{:S(2)}, u32[]{:S(2)}) collective-permute-start(bf16[7,384,128]{2,1,0:T(8,128)(2,1)S(1)} %pad_maximum_fusion.1), channel_id=1, source_target_pairs={{4,0},{8,4},{12,8},{16,12},{20,16},{24,20},{28,24},{0,28},{5,1},{9... | collective-permute-start | bytes 2064392 | tf_op jit(solution)/shard_map/ppermute | solution.py:354
  119.7 56.2 %collective-permute-start.13 = (bf16[16,96,128]{2,1,0:T(8,128)(2,1)S(1)}, bf16[16,96,128]{2,1,0:T(8,128)(2,1)S(1)}, u32[]{:S(2)}, u32[]{:S(2)}) collective-permute-start(bf16[16,96,128]{2,1,0:T(8,128)(2,1)S(1)} %get-tuple-element.26), channel_id=1, source_target_pairs={{0,3},{1,0},{2,1},{3,2},{4,7},{5,4},{6,5},{7,6},{8,11},{9,8},{10,9... | collective-permute-start | bytes 1179656 | tf_op jit(solution)/shard_map/ppermute | solution.py:359
  131.4 44.6 %collective-permute-start.14 = (bf16[16,96,128]{2,1,0:T(8,128)(2,1)S(1)}, bf16[16,96,128]{2,1,0:T(8,128)(2,1)S(1)}, u32[]{:S(2)}, u32[]{:S(2)}) collective-permute-start(bf16[16,96,128]{2,1,0:T(8,128)(2,1)S(1)} %get-tuple-element.27), channel_id=1, source_target_pairs={{0,2},{1,3},{2,0},{3,1},{4,6},{5,7},{6,4},{7,5},{8,10},{9,11},{10,... | collective-permute-start | bytes 1179656 | tf_op jit(solution)/shard_map/ppermute | solution.py:359
  131.4 44.6 %collective-permute-start.15 = (bf16[16,96,128]{2,1,0:T(8,128)(2,1)S(1)}, bf16[16,96,128]{2,1,0:T(8,128)(2,1)S(1)}, u32[]{:S(2)}, u32[]{:S(2)}) collective-permute-start(bf16[16,96,128]{2,1,0:T(8,128)(2,1)S(1)} %get-tuple-element.28), channel_id=1, source_target_pairs={{0,1},{1,2},{2,3},{3,0},{4,5},{5,6},{6,7},{7,4},{8,9},{9,10},{10,1... | collective-permute-start | bytes 1179656 | tf_op jit(solution)/shard_map/ppermute | solution.py:359
  171.5 12.9 %collective-permute-start.8 = (bf16[16,96,128]{2,1,0:T(8,128)(2,1)S(1)}, bf16[16,96,128]{2,1,0:T(8,128)(2,1)S(1)}, u32[]{:S(2)}, u32[]{:S(2)}) collective-permute-start(bf16[16,96,128]{2,1,0:T(8,128)(2,1)S(1)} %get-tuple-element.22), channel_id=1, source_target_pairs={{0,3},{1,0},{2,1},{3,2},{4,7},{5,4},{6,5},{7,6},{8,11},{9,8},{10,9... | collective-permute-start | bytes 1179656 | tf_op jit(solution)/shard_map/ppermute | solution.py:359
  174.8 33.5 %collective-permute-start.9 = (bf16[16,96,128]{2,1,0:T(8,128)(2,1)S(1)}, bf16[16,96,128]{2,1,0:T(8,128)(2,1)S(1)}, u32[]{:S(2)}, u32[]{:S(2)}) collective-permute-start(bf16[16,96,128]{2,1,0:T(8,128)(2,1)S(1)} %get-tuple-element.23), channel_id=1, source_target_pairs={{0,2},{1,3},{2,0},{3,1},{4,6},{5,7},{6,4},{7,5},{8,10},{9,11},{10,... | collective-permute-start | bytes 1179656 | tf_op jit(solution)/shard_map/ppermute | solution.py:359
  175.9 32.4 %collective-permute-start.10 = (bf16[16,96,128]{2,1,0:T(8,128)(2,1)S(1)}, bf16[16,96,128]{2,1,0:T(8,128)(2,1)S(1)}, u32[]{:S(2)}, u32[]{:S(2)}) collective-permute-start(bf16[16,96,128]{2,1,0:T(8,128)(2,1)S(1)} %get-tuple-element.24), channel_id=1, source_target_pairs={{0,1},{1,2},{2,3},{3,0},{4,5},{5,6},{6,7},{7,4},{8,9},{9,10},{10,1... | collective-permute-start | bytes 1179656 | tf_op jit(solution)/shard_map/ppermute | solution.py:359
  184.4 23.9 %copy-start.7 = (bf16[16,96,128]{2,1,0:T(8,128)(2,1)}, bf16[16,96,128]{2,1,0:T(8,128)(2,1)S(1)}, u32[]{:S(2)}) copy-start(bf16[16,96,128]{2,1,0:T(8,128)(2,1)S(1)} %collective-permute-done.8.refs_1_) | copy-start | bytes 1179652
  (12 other events, 10.8 us)

commit v2 on v1

--- a/solution.py
+++ b/solution.py
@@ -126,7 +126,7 @@
 def pack(density, place, shift, part, devices, parts):
     share, rows, columns = density.shape
     tiles = columns // LANES
-    step = 32
+    step = share
 
     def tile(offset):
         def index(block, place_ref):
@@ -187,97 +187,106 @@
 
 def steps_kernel(devices, *refs):
     blocks = refs[:devices]
-    above, below, kernel, turn, keep, by_row, by_column, choose = refs[devices : devices + 8]
-    outs = refs[devices + 8 : 2 * devices + 8]
-    first, second, advected = refs[2 * devices + 8 :]
+    above, below, kernel, turn, coefficients = refs[devices : devices + 5]
+    outs = refs[devices + 5 : 2 * devices + 5]
+    buffers = refs[2 * devices + 5 : 2 * devices + 7]
+    waiting = refs[2 * devices + 7 :]
     share = blocks[0].shape[1]
     number = share * devices
     rows = outs[0].shape[0]
-
-    def turned_back(value, slot):
-        return pltpu.roll(value.astype(jnp.float32), (LANES - SLOT * slot) % LANES, 1).astype(jnp.bfloat16)
-
-    for index in range(rows + 2 * REACH):
-        row = index - REACH
-        slot = row % GROUP
-        if row < 0:
-            first[index, :, :LANES] = above[index]
-            first[index, :, LANES:] = turned_back(above[REACH], slot)
-        elif row >= rows:
-            first[index, :, :LANES] = below[1 + row - rows]
-            first[index, :, LANES:] = turned_back(below[0], slot)
-        else:
-            for part in range(devices):
-                span = slice(part * share, (part + 1) * share)
-                first[index, span, :LANES] = blocks[part][1 + row]
-                first[index, span, LANES:] = turned_back(blocks[part][0 if row < GROUP else rows + 1], slot)
-
-    block = 48
-
-    def advect(source, row, tiles, target, column):
-        lane = lax.broadcasted_iota(jnp.int32, (block, LANES), 1)
-        for start in range(0, number, block):
-            span = slice(start, start + block)
-            forward_row = choose[0, span] > 0
-            forward_column = choose[1, span] > 0
-            depth = jnp.where(forward_column, lane, LANES - 1 - lane)
-            edge_one, edge_two = depth < 1, depth < 2
-            centres, ones, twos = [], [], []
-            for tile in range(2):
-                centre = source[row + 2, span, tile * LANES : (tile + 1) * LANES].astype(jnp.float32)
-                centres.append(centre)
-                ones.append(jnp.where(forward_column, pltpu.roll(centre, 1, 1), pltpu.roll(centre, LANES - 1, 1)))
-                twos.append(jnp.where(forward_column, pltpu.roll(centre, 2, 1), pltpu.roll(centre, LANES - 2, 1)))
+    tiles = number // LANES
+
+    def transposed(value_of):
+        return jnp.concatenate([value_of(part).astype(jnp.float32) for part in range(devices)], 0).T
+
+    def piece(ref, index, part):
+        return ref[index, part * share : (part + 1) * share]
+
+    def fill(first, last, value_of):
+        for row in range(first, last):
+            cells = transposed(lambda part: value_of(row, part))
+            for tile in range(tiles):
+                buffers[0][row + REACH, tile, 2 * GROUP : 2 * GROUP + LANES] = cells[
+                    :, tile * LANES : (tile + 1) * LANES
+                ]
+
+    def fill_sides(first, last, value_of):
+        cells = transposed(value_of)
+        for row in range(first, last):
+            slot = row % GROUP
+            left, right = (SLOT * slot - GROUP) % LANES, SLOT * slot
             for tile in range(tiles):
                 lanes = slice(tile * LANES, (tile + 1) * LANES)
-
-                def at(offset):
-                    return source[row + 2 + offset, span, lanes].astype(jnp.float32)
-
-                row_one = jnp.where(forward_row, at(-1), at(1))
-                row_two = jnp.where(forward_row, at(-2), at(2))
-                column_one = jnp.where(edge_one, ones[1 - tile], ones[tile])
-                column_two = jnp.where(edge_two, twos[1 - tile], twos[tile])
+                buffers[0][row + REACH, tile, GROUP : 2 * GROUP] = cells[left : left + GROUP, lanes]
+                buffers[0][row + REACH, tile, 2 * GROUP + LANES : 3 * GROUP + LANES] = cells[
+                    right : right + GROUP, lanes
+                ]
+
+    fill(-REACH, 0, lambda row, part: piece(above, row + REACH, part))
+    fill(0, rows, lambda row, part: blocks[part][1 + row])
+    fill(rows, rows + REACH, lambda row, part: piece(below, 1 + row - rows, part))
+    fill_sides(-REACH, 0, lambda part: piece(above, REACH, part))
+    fill_sides(0, GROUP, lambda part: blocks[part][0])
+    fill_sides(GROUP, rows, lambda part: blocks[part][rows + 1])
+    fill_sides(rows, rows + REACH, lambda part: piece(below, 0, part))
+
+    def advect(source, index, start, length, target):
+        for tile in range(tiles):
+            lanes = slice(tile * LANES, (tile + 1) * LANES)
+            keep, by_row, by_column, row_sign, column_sign = (coefficients[k : k + 1, lanes] for k in range(5))
+            forward_row = jnp.broadcast_to(row_sign, (length, LANES)) > 0
+            forward_column = jnp.broadcast_to(column_sign, (length, LANES)) > 0
+            for half in range(2):
+
+                def at(row, column):
+                    return source[index + half + row, tile, start + column : start + column + length]
+
+                row_one = jnp.where(forward_row, at(-1, 0), at(1, 0))
+                row_two = jnp.where(forward_row, at(-2, 0), at(2, 0))
+                column_one = jnp.where(forward_column, at(0, -1), at(0, 1))
+                column_two = jnp.where(forward_column, at(0, -2), at(0, 2))
                 value = (
-                    keep[span] * centres[tile]
-                    + by_row[span] * (row_one - 0.25 * row_two)
-                    + by_column[span] * (column_one - 0.25 * column_two)
+                    keep * at(0, 0)
+                    + by_row * (row_one - 0.25 * row_two)
+                    + by_column * (column_one - 0.25 * column_two)
                 )
-                target[span, column + tile * LANES : column + (tile + 1) * LANES] = value.astype(jnp.bfloat16)
+                target[half * length : (half + 1) * length, lanes] = value.astype(jnp.bfloat16)
 
     def rotate(values):
-        potential = jnp.dot(kernel[...], values[...], preferred_element_type=jnp.float32)
-        drifted = (values[...].astype(jnp.float32) * (1.0 + potential)).astype(jnp.bfloat16)
-        turned = jnp.dot(turn[...], drifted, preferred_element_type=jnp.float32)
-        return (values[...].astype(jnp.float32) + rotation_rate * turned).astype(jnp.bfloat16)
-
-    buffers = [first, second]
-    for step in range(TIME_STEPS - 1):
+        potential = jnp.dot(values, kernel[...], preferred_element_type=jnp.float32)
+        drifted = (values.astype(jnp.float32) * (1.0 + potential)).astype(jnp.bfloat16)
+        turned = jnp.dot(drifted, turn[...], preferred_element_type=jnp.float32)
+        return (values.astype(jnp.float32) + rotation_rate * turned).astype(jnp.bfloat16)
+
+    for step in range(TIME_STEPS):
         source, target = buffers[step % 2], buffers[(step + 1) % 2]
-
-        @pl.loop(0, (rows + 2 * REACH - 4 * (step + 1)) // 2)
-        def _(pair):
-            row = 2 * pair
+        last = step == TIME_STEPS - 1
+        start, length = (2 * GROUP, LANES) if last else (GROUP, LANES + 2 * GROUP)
+        low, pairs = 2 * (step + 1), rows // 2 + REACH - 2 * (step + 1)
+
+        def finish(slot, index):
+            result = rotate(waiting[slot][: 2 * length]).astype(jnp.float32)
             for half in range(2):
-                advect(source, row + half, 2, advected.at[half], 0)
-            for half in range(2):
-                target[row + half] = rotate(advected.at[half])
-
-    source = buffers[(TIME_STEPS - 1) % 2]
-
-    @pl.loop(0, rows // 4)
-    def _(quad):
-        row = 4 * quad
-        for half in range(2):
-            for side in range(2):
-                advect(source, row + 2 * half + side, 1, advected.at[half], side * LANES)
-        for half in range(2):
-            result = rotate(advected.at[half])
-            for side in range(2):
-                for part in range(devices):
-                    outs[part][row + 2 * half + side] = result[
-                        part * share : (part + 1) * share, side * LANES : (side + 1) * LANES
-                    ]
+                cells = result[half * length : (half + 1) * length]
+                if last:
+                    back = cells.T.astype(jnp.bfloat16)
+                    for part in range(devices):
+                        outs[part][index - REACH + half] = back[part * share : (part + 1) * share]
+                else:
+                    for tile in range(tiles):
+                        target[index + half, tile, start : start + length] = cells[
+                            :, tile * LANES : (tile + 1) * LANES
+                        ]
+
+        advect(source, low, start, length, waiting[0])
+
+        @pl.loop(0, pairs // 2)
+        def _(turn_index):
+            index = low + 4 * turn_index
+            advect(source, index + 2, start, length, waiting[1])
+            finish(0, index)
+            advect(source, jnp.minimum(index + 4, low + 2 * pairs - 2), start, length, waiting[0])
+            finish(1, index + 2)
 
 
 def three_steps(blocks, above, below, kernel, turn, coefficients):
@@ -285,18 +294,17 @@
     rows, share, _ = blocks[0].shape
     rows -= 2
     number = share * devices
-    cells = (rows + 2 * REACH) * 2 * LANES
+    cells = (rows + 2 * REACH) * LANES
     vmem = pl.BlockSpec(memory_space=pltpu.VMEM)
-    operands = (*blocks, above, below, kernel, turn, *coefficients)
+    operands = (*blocks, above, below, kernel, turn, coefficients)
     return pl.pallas_call(
         functools.partial(steps_kernel, devices),
         in_specs=[vmem] * len(operands),
         out_specs=[vmem] * devices,
         out_shape=[jax.ShapeDtypeStruct((rows, share, LANES), jnp.bfloat16)] * devices,
         scratch_shapes=[
-            pltpu.VMEM((rows + 2 * REACH, number, 2 * LANES), jnp.bfloat16),
-            pltpu.VMEM((rows + 2 * REACH - 4, number, 2 * LANES), jnp.bfloat16),
-            pltpu.VMEM((2, number, 2 * LANES), jnp.bfloat16),
+            *[pltpu.VMEM((rows + 2 * REACH, number // LANES, LANES + 4 * GROUP, LANES), jnp.float32)] * 2,
+            *[pltpu.VMEM((2 * (LANES + 2 * GROUP), number), jnp.bfloat16)] * 2,
         ],
         compiler_params=pltpu.CompilerParams(vmem_limit_bytes=48 * 2**20),
         cost_estimate=pl.CostEstimate(
@@ -326,15 +334,16 @@
     kernel = turned(turned(kernel, 0), 1)
     signs, speeds = turned(signs, 1), turned(speeds, 1)
 
-    def spread(value):
-        return jnp.broadcast_to(value[..., None], value.shape + (LANES,))
-
-    coefficients = (
-        spread(1.0 - 1.5 * (speeds[0] + speeds[1])),
-        spread(2.0 * speeds[0]),
-        spread(2.0 * speeds[1]),
-        spread((signs == 1).astype(jnp.float32)),
+    coefficients = jnp.stack(
+        [
+            1.0 - 1.5 * (speeds[0] + speeds[1]),
+            2.0 * speeds[0],
+            2.0 * speeds[1],
+            (signs[0] == 1).astype(jnp.float32),
+            (signs[1] == 1).astype(jnp.float32),
+        ]
     )
+    kernel, turn = kernel.T, turn.T
 
     size = lax.axis_size("gx")
     up = [(i, (i + 1) % size) for i in range(size)]
@@ -350,6 +359,8 @@
             lax.ppermute(blocks[shift], "ao", [(i, (i + shift) % devices) for i in range(devices)])
             for shift in range(1, devices)
         ]
+        if results:
+            arrived, _ = lax.optimization_barrier((arrived, results[-1]))
         above = lax.ppermute(jnp.concatenate([block[-(REACH + 1) :] for block in arrived], 1), "gx", up)
         below = lax.ppermute(jnp.concatenate([block[: REACH + 1] for block in arrived], 1), "gx", down)
         results.append(three_steps(arrived, above, below, kernel, turn, coefficients))

time: 214 us -> 169 us (0.79)
  Pallas kernels: 111 us -> 65.9 us
  starting transfers between devices: 41.5 us -> 53.8 us
  waiting for transfers between devices: 53.2 us -> 42.3 us
    pallas_call x2, Pallas kernels: 76 us -> 35.8 us  [three_steps(): pl.pallas_call(functools.partial(steps_kernel, devices), in_specs=[vmem]...]
    ppermute x6, starting transfers between devices: 16.7 us -> 30.2 us  [blocked(): lax.ppermute(result[shift], 'ao', [(i, (i - shift) % devices) for i in ra...]
    ppermute x6, waiting for transfers between devices: 26.1 us -> 13.6 us  [blocked(): lax.ppermute(blocks[shift], 'ao', [(i, (i + shift) % devices) for i in ra...]
    pallas_call x8, Pallas kernels: 26.1 us -> 21.4 us  [pack(): pl.pallas_call(pack_kernel, grid_spec=pltpu.PrefetchScalarGridSpec(num_sc...]
    unnamed x40 -> x38, local copies, waits for them, and re-layouts: 4.72 us -> 3.54 us
  transfers between devices with their start and end apart: 16 -> 16, of which waited for: 5 -> 7; matrix products, arithmetic and copies ran while one was open for 1% -> 2% of each run, Pallas kernels for 48% -> 35%
where the time goes in v2:
time: 169 us
  Pallas kernels  65.9 us (39%)
  starting transfers between devices  53.8 us (32%)
  waiting for transfers between devices  42.3 us (25%)
  local copies, waits for them, and re-layouts  4.51 us (3%)
  other arithmetic  1.74 us (1%)
    pallas_call x2, Pallas kernels, three_steps(): pl.pallas_call(functools.partial(steps_kernel, devices), in_specs=[vmem]...  35.8 us
    ppermute x6, starting transfers between devices, blocked(): lax.ppermute(result[shift], 'ao', [(i, (i - shift) % devices) for i in ra...  30.2 us
    ppermute x6, waiting for transfers between devices, blocked(): lax.ppermute(result[shift], 'ao', [(i, (i - shift) % devices) for i in ra...  28.2 us
    pallas_call x8, Pallas kernels, pack(): pl.pallas_call(pack_kernel, grid_spec=pltpu.PrefetchScalarGridSpec(num_sc...  21.4 us
    ppermute x6, starting transfers between devices, blocked(): lax.ppermute(blocks[shift], 'ao', [(i, (i + shift) % devices) for i in ra...  18.1 us
    ppermute x6, waiting for transfers between devices, blocked(): lax.ppermute(blocks[shift], 'ao', [(i, (i + shift) % devices) for i in ra...  13.6 us
    pallas_call x2, Pallas kernels, unpack(): pl.pallas_call(functools.partial(unpack_kernel, devices), grid_spec=pltpu...  8.69 us
    ppermute x2, starting transfers between devices, blocked(): lax.ppermute(jnp.concatenate([block[:REACH + 1] for block in arrived], 1)...  5.35 us
  transfers between devices with their start and end apart: 16, of which 7 were waited for; matrix products, arithmetic and copies ran while one was open for 2% of the time, Pallas kernels for 35%

profile of v2, /device:TPU:0, one launch (start us, length us, event | category | flops | bytes accessed | tf_op | source)
XLA Modules:
  0.0 168.6 jit_solution(15670884242006797714)
XLA Ops:
  0.0 2.7 %pack.14 = bf16[18,96,128]{2,1,0:T(8,128)(2,1)} custom-call(s32[1]{0:T(128)} %bitcast.place, bf16[96,16,1024]{2,1,0:T(8,128)(2,1)} %after_ref.15, bf16[96,16,1024]{2,1,0:T(8,128)(2,1)} %after_ref.15, bf16[96,16,1024]{2,1,0:T(8,128)(2,1)} %after_ref.15), custom_call_target="tpu_custom_call" | custom-call | tf_op jit(solution)/shard_map/pack/pallas_call | solution.py:138
  2.7 4.0 %collective-permute-start.1 = (bf16[18,96,128]{2,1,0:T(8,128)(2,1)}, bf16[18,96,128]{2,1,0:T(8,128)(2,1)S(1)}, u32[]{:S(2)}, u32[]{:S(2)}) collective-permute-start(bf16[18,96,128]{2,1,0:T(8,128)(2,1)} %pack.14), channel_id=1, source_target_pairs={{0,2},{1,3},{2,0},{3,1},{4,6},{5,7},{6,4},{7,5},{8,10},{9,11},{10,... | collective-permute-start | bytes 1327112 | tf_op jit(solution)/shard_map/ppermute | solution.py:359
  6.7 2.7 %pack.15 = bf16[18,96,128]{2,1,0:T(8,128)(2,1)} custom-call(s32[1]{0:T(128)} %bitcast.place, bf16[96,16,1024]{2,1,0:T(8,128)(2,1)} %after_ref.15, bf16[96,16,1024]{2,1,0:T(8,128)(2,1)} %after_ref.15, bf16[96,16,1024]{2,1,0:T(8,128)(2,1)} %after_ref.15), custom_call_target="tpu_custom_call" | custom-call | tf_op jit(solution)/shard_map/pack/pallas_call | solution.py:138
  10.7 2.7 %pack.13 = bf16[18,96,128]{2,1,0:T(8,128)(2,1)} custom-call(s32[1]{0:T(128)} %bitcast.place, bf16[96,16,1024]{2,1,0:T(8,128)(2,1)} %after_ref.15, bf16[96,16,1024]{2,1,0:T(8,128)(2,1)} %after_ref.15, bf16[96,16,1024]{2,1,0:T(8,128)(2,1)} %after_ref.15), custom_call_target="tpu_custom_call" | custom-call | tf_op jit(solution)/shard_map/pack/pallas_call | solution.py:138
  14.1 2.7 %pack.12.refs_0_ = bf16[18,96,128]{2,1,0:T(8,128)(2,1)} custom-call(s32[1]{0:T(128)} %bitcast.place, bf16[96,16,1024]{2,1,0:T(8,128)(2,1)} %after_ref.15, bf16[96,16,1024]{2,1,0:T(8,128)(2,1)} %after_ref.15, bf16[96,16,1024]{2,1,0:T(8,128)(2,1)} %after_ref.15), custom_call_target="tpu_custom_call" | custom-call | tf_op jit(solution)/shard_map/pack/pallas_call | solution.py:138
  16.8 2.7 %pack.11 = bf16[18,96,128]{2,1,0:T(8,128)(2,1)} custom-call(s32[1]{0:T(128)} %bitcast.place, bf16[96,16,1024]{2,1,0:T(8,128)(2,1)} %after_ref.15, bf16[96,16,1024]{2,1,0:T(8,128)(2,1)} %after_ref.15, bf16[96,16,1024]{2,1,0:T(8,128)(2,1)} %after_ref.15), custom_call_target="tpu_custom_call" | custom-call | tf_op jit(solution)/shard_map/pack/pallas_call | solution.py:138
  19.5 2.7 %pack.10 = bf16[18,96,128]{2,1,0:T(8,128)(2,1)} custom-call(s32[1]{0:T(128)} %bitcast.place, bf16[96,16,1024]{2,1,0:T(8,128)(2,1)} %after_ref.15, bf16[96,16,1024]{2,1,0:T(8,128)(2,1)} %after_ref.15, bf16[96,16,1024]{2,1,0:T(8,128)(2,1)} %after_ref.15), custom_call_target="tpu_custom_call" | custom-call | tf_op jit(solution)/shard_map/pack/pallas_call | solution.py:138
  22.1 2.7 %pack.9 = bf16[18,96,128]{2,1,0:T(8,128)(2,1)} custom-call(s32[1]{0:T(128)} %bitcast.place, bf16[96,16,1024]{2,1,0:T(8,128)(2,1)} %after_ref.15, bf16[96,16,1024]{2,1,0:T(8,128)(2,1)} %after_ref.15, bf16[96,16,1024]{2,1,0:T(8,128)(2,1)} %after_ref.15), custom_call_target="tpu_custom_call" | custom-call | tf_op jit(solution)/shard_map/pack/pallas_call | solution.py:138
  24.8 2.7 %pack.8.refs_0_ = bf16[18,96,128]{2,1,0:T(8,128)(2,1)} custom-call(s32[1]{0:T(128)} %bitcast.place, bf16[96,16,1024]{2,1,0:T(8,128)(2,1)} %after_ref.15, bf16[96,16,1024]{2,1,0:T(8,128)(2,1)} %after_ref.15, bf16[96,16,1024]{2,1,0:T(8,128)(2,1)} %after_ref.15), custom_call_target="tpu_custom_call" | custom-call | tf_op jit(solution)/shard_map/pack/pallas_call | solution.py:138
  29.8 9.3 %collective-permute-done.2.refs_3_ = bf16[18,96,128]{2,1,0:T(8,128)(2,1)S(1)} collective-permute-done((bf16[18,96,128]{2,1,0:T(8,128)(2,1)}, bf16[18,96,128]{2,1,0:T(8,128)(2,1)S(1)}, u32[]{:S(2)}, u32[]{:S(2)}) %collective-permute-start.2) | collective-permute-done | bytes 442400 | tf_op jit(solution)/shard_map/ppermute | solution.py:359
  39.3 2.7 %collective-permute-start.7 = (bf16[7,384,128]{2,1,0:T(8,128)(2,1)S(1)}, bf16[7,384,128]{2,1,0:T(8,128)(2,1)S(1)}, u32[]{:S(2)}, u32[]{:S(2)}) collective-permute-start(bf16[7,384,128]{2,1,0:T(8,128)(2,1)S(1)} %pad_maximum_fusion.1), channel_id=1, source_target_pairs={{4,0},{8,4},{12,8},{16,12},{20,16},{24,20},{28,24},{0,28},{5,1},{9... | collective-permute-start | bytes 2064392 | tf_op jit(solution)/shard_map/ppermute | solution.py:365
  43.4 7.3 %collective-permute-start.3 = (bf16[18,96,128]{2,1,0:T(8,128)(2,1)S(1)}, bf16[18,96,128]{2,1,0:T(8,128)(2,1)S(1)}, u32[]{:S(2)}, u32[]{:S(2)}) collective-permute-start(bf16[18,96,128]{2,1,0:T(8,128)(2,1)S(1)} %copy-done.6), channel_id=1, source_target_pairs={{0,1},{1,2},{2,3},{3,0},{4,5},{5,6},{6,7},{7,4},{8,9},{9,10},{10,1... | collective-permute-start | bytes 1327112 | tf_op jit(solution)/shard_map/ppermute | solution.py:359
  50.7 1.9 %collective-permute-start.4 = (bf16[18,96,128]{2,1,0:T(8,128)(2,1)S(1)}, bf16[18,96,128]{2,1,0:T(8,128)(2,1)S(1)}, u32[]{:S(2)}, u32[]{:S(2)}) collective-permute-start(bf16[18,96,128]{2,1,0:T(8,128)(2,1)S(1)} %copy-done.5), channel_id=1, source_target_pairs={{0,2},{1,3},{2,0},{3,1},{4,6},{5,7},{6,4},{7,5},{8,10},{9,11},{10,... | collective-permute-start | bytes 1327112 | tf_op jit(solution)/shard_map/ppermute | solution.py:359
  52.7 2.8 %collective-permute-start.5 = (bf16[18,96,128]{2,1,0:T(8,128)(2,1)S(1)}, bf16[18,96,128]{2,1,0:T(8,128)(2,1)S(1)}, u32[]{:S(2)}, u32[]{:S(2)}) collective-permute-start(bf16[18,96,128]{2,1,0:T(8,128)(2,1)S(1)} %copy-done.4), channel_id=1, source_target_pairs={{0,3},{1,0},{2,1},{3,2},{4,7},{5,4},{6,5},{7,6},{8,11},{9,8},{10,9... | collective-permute-start | bytes 1327112 | tf_op jit(solution)/shard_map/ppermute | solution.py:359
  56.0 17.9 %three_steps.2 = (bf16[16,96,128]{2,1,0:T(8,128)(2,1)S(1)}, bf16[16,96,128]{2,1,0:T(8,128)(2,1)S(1)}, bf16[16,96,128]{2,1,0:T(8,128)(2,1)S(1)}, bf16[16,96,128]{2,1,0:T(8,128)(2,1)S(1)}) custom-call(bf16[18,96,128]{2,1,0:T(8,128)(2,1)S(1)} %copy-done.1, bf16[18,96,128]{2,1,0:T(8,128)(2,1)S(1)} %collective-permute-done.refs_1_, ...), custom_call_target="tpu_custom_call" | custom-call | flops 6341787648 | bytes 8388608 | tf_op jit(solution)/shard_map/three_steps/pallas_call | solution.py:300
  73.9 4.0 %collective-permute-done.4.refs_2_ = bf16[18,96,128]{2,1,0:T(8,128)(2,1)S(1)} collective-permute-done((bf16[18,96,128]{2,1,0:T(8,128)(2,1)S(1)}, bf16[18,96,128]{2,1,0:T(8,128)(2,1)S(1)}, u32[]{:S(2)}, u32[]{:S(2)}) %collective-permute-start.4) | collective-permute-done | bytes 442400 | tf_op jit(solution)/shard_map/ppermute | solution.py:359
  78.6 2.7 %collective-permute-start.9 = (bf16[7,384,128]{2,1,0:T(8,128)(2,1)S(1)}, bf16[7,384,128]{2,1,0:T(8,128)(2,1)S(1)}, u32[]{:S(2)}, u32[]{:S(2)}) collective-permute-start(bf16[7,384,128]{2,1,0:T(8,128)(2,1)S(1)} %pad_maximum_fusion.3), channel_id=1, source_target_pairs={{4,0},{8,4},{12,8},{16,12},{20,16},{24,20},{28,24},{0,28},{5,1},{9... | collective-permute-start | bytes 2064392 | tf_op jit(solution)/shard_map/ppermute | solution.py:365
  81.3 14.6 %collective-permute-start.13 = (bf16[16,96,128]{2,1,0:T(8,128)(2,1)S(1)}, bf16[16,96,128]{2,1,0:T(8,128)(2,1)S(1)}, u32[]{:S(2)}, u32[]{:S(2)}) collective-permute-start(bf16[16,96,128]{2,1,0:T(8,128)(2,1)S(1)} %get-tuple-element.26), channel_id=1, source_target_pairs={{0,3},{1,0},{2,1},{3,2},{4,7},{5,4},{6,5},{7,6},{8,11},{9,8},{10,9... | collective-permute-start | bytes 1179656 | tf_op jit(solution)/shard_map/ppermute | solution.py:370
  96.5 17.9 %three_steps.3 = (bf16[16,96,128]{2,1,0:T(8,128)(2,1)S(1)}, bf16[16,96,128]{2,1,0:T(8,128)(2,1)S(1)}, bf16[16,96,128]{2,1,0:T(8,128)(2,1)S(1)}, bf16[16,96,128]{2,1,0:T(8,128)(2,1)S(1)}) custom-call(bf16[18,96,128]{2,1,0:T(8,128)(2,1)S(1)} %copy-done, bf16[18,96,128]{2,1,0:T(8,128)(2,1)S(1)} %collective-permute-done.3.refs_1_, ...), custom_call_target="tpu_custom_call" | custom-call | flops 6341787648 | bytes 8388608 | tf_op jit(solution)/shard_map/three_steps/pallas_call | solution.py:300
  115.1 14.4 %collective-permute-start.10 = (bf16[16,96,128]{2,1,0:T(8,128)(2,1)S(1)}, bf16[16,96,128]{2,1,0:T(8,128)(2,1)S(1)}, u32[]{:S(2)}, u32[]{:S(2)}) collective-permute-start(bf16[16,96,128]{2,1,0:T(8,128)(2,1)S(1)} %get-tuple-element.34), channel_id=1, source_target_pairs={{0,3},{1,0},{2,1},{3,2},{4,7},{5,4},{6,5},{7,6},{8,11},{9,8},{10,9... | collective-permute-start | bytes 1179656 | tf_op jit(solution)/shard_map/ppermute | solution.py:370
  130.9 4.3 %unpack.2.refs_4_ = bf16[96,16,1024]{2,1,0:T(8,128)(2,1)} custom-call(s32[1]{0:T(128)} %bitcast.place, bf16[16,96,128]{2,1,0:T(8,128)(2,1)} %copy-done.3, bf16[16,96,128]{2,1,0:T(8,128)(2,1)} %copy-done.10, bf16[16,96,128]{2,1,0:T(8,128)(2,1)} %copy-done.11, bf16[16,96,128]{2,1,0:T(8,128)(2,1)} %collective-permute-done.15.refs_3_), custom_call_target="tpu_custom_call" | custom-call | tf_op jit(solution)/shard_map/unpack/pallas_call | solution.py:173
  135.2 3.7 %collective-permute-done.10.refs_1_ = bf16[16,96,128]{2,1,0:T(8,128)(2,1)S(1)} collective-permute-done((bf16[16,96,128]{2,1,0:T(8,128)(2,1)S(1)}, bf16[16,96,128]{2,1,0:T(8,128)(2,1)S(1)}, u32[]{:S(2)}, u32[]{:S(2)}) %collective-permute-start.10) | collective-permute-done | bytes 393248 | tf_op jit(solution)/shard_map/ppermute | solution.py:370
  138.9 24.5 %collective-permute-done.11.refs_2_ = bf16[16,96,128]{2,1,0:T(8,128)(2,1)S(1)} collective-permute-done((bf16[16,96,128]{2,1,0:T(8,128)(2,1)S(1)}, bf16[16,96,128]{2,1,0:T(8,128)(2,1)S(1)}, u32[]{:S(2)}, u32[]{:S(2)}) %collective-permute-start.11) | collective-permute-done | bytes 393248 | tf_op jit(solution)/shard_map/ppermute | solution.py:370
  164.3 4.3 %unpack.3 = bf16[96,16,1024]{2,1,0:T(8,128)(2,1)} custom-call(s32[1]{0:T(128)} %bitcast.place, bf16[16,96,128]{2,1,0:T(8,128)(2,1)} %copy-done.2, bf16[16,96,128]{2,1,0:T(8,128)(2,1)} %copy-done.7, bf16[16,96,128]{2,1,0:T(8,128)(2,1)} %copy-done.8, bf16[16,96,128]{2,1,0:T(8,128)(2,1)} %copy-done.9, ...), custom_call_target="tpu_custom_call", output_to_operand_aliasing={{}: (5, {})} | custom-call | tf_op jit(solution)/shard_map/unpack/pallas_call | solution.py:173
  (89 shorter events, 10.4 us)
Async XLA Ops:
  2.7 27.0 %collective-permute-start.1 = (bf16[18,96,128]{2,1,0:T(8,128)(2,1)}, bf16[18,96,128]{2,1,0:T(8,128)(2,1)S(1)}, u32[]{:S(2)}, u32[]{:S(2)}) collective-permute-start(bf16[18,96,128]{2,1,0:T(8,128)(2,1)} %pack.14), channel_id=1, source_target_pairs={{0,2},{1,3},{2,0},{3,1},{4,6},{5,7},{6,4},{7,5},{8,10},{9,11},{10,... | collective-permute-start | bytes 1327112 | tf_op jit(solution)/shard_map/ppermute | solution.py:359
  9.4 4.7 %copy-start.13 = (s32[384,6]{0,1:T(8,128)S(1)}, s32[384,6]{0,1:T(8,128)}, u32[]{:S(2)}) copy-start(s32[384,6]{0,1:T(8,128)} %param.9) | copy-start | bytes 27652
  9.4 29.6 %collective-permute-start.2 = (bf16[18,96,128]{2,1,0:T(8,128)(2,1)}, bf16[18,96,128]{2,1,0:T(8,128)(2,1)S(1)}, u32[]{:S(2)}, u32[]{:S(2)}) collective-permute-start(bf16[18,96,128]{2,1,0:T(8,128)(2,1)} %pack.15), channel_id=1, source_target_pairs={{0,3},{1,0},{2,1},{3,2},{4,7},{5,4},{6,5},{7,6},{8,11},{9,8},{10,9... | collective-permute-start | bytes 1327112 | tf_op jit(solution)/shard_map/ppermute | solution.py:359
  13.4 25.6 %collective-permute-start = (bf16[18,96,128]{2,1,0:T(8,128)(2,1)}, bf16[18,96,128]{2,1,0:T(8,128)(2,1)S(1)}, u32[]{:S(2)}, u32[]{:S(2)}) collective-permute-start(bf16[18,96,128]{2,1,0:T(8,128)(2,1)} %pack.13), channel_id=1, source_target_pairs={{0,1},{1,2},{2,3},{3,0},{4,5},{5,6},{6,7},{7,4},{8,9},{9,10},{10,1... | collective-permute-start | bytes 1327112 | tf_op jit(solution)/shard_map/ppermute | solution.py:359
  24.8 3.1 %copy-start.12 = (bf16[384,384]{1,0:T(8,128)(2,1)S(1)}, bf16[384,384]{1,0:T(8,128)(2,1)}, u32[]{:S(2)}) copy-start(bf16[384,384]{1,0:T(8,128)(2,1)} %param.7) | copy-start | bytes 884740
  24.8 3.7 %copy-start.14 = (s32[384,6]{0,1:T(8,128)S(1)}, s32[384,6]{0,1:T(8,128)}, u32[]{:S(2)}) copy-start(s32[384,6]{0,1:T(8,128)} %param.8) | copy-start | bytes 27652
  39.1 16.6 %collective-permute-start.6 = (bf16[7,384,128]{2,1,0:T(8,128)(2,1)S(1)}, bf16[7,384,128]{2,1,0:T(8,128)(2,1)S(1)}, u32[]{:S(2)}, u32[]{:S(2)}) collective-permute-start(bf16[7,384,128]{2,1,0:T(8,128)(2,1)S(1)} %pad_maximum_fusion), channel_id=1, source_target_pairs={{0,4},{4,8},{8,12},{12,16},{16,20},{20,24},{24,28},{28,0},{1,5},{5... | collective-permute-start | bytes 2064392 | tf_op jit(solution)/shard_map/ppermute | solution.py:364
  39.3 16.7 %collective-permute-start.7 = (bf16[7,384,128]{2,1,0:T(8,128)(2,1)S(1)}, bf16[7,384,128]{2,1,0:T(8,128)(2,1)S(1)}, u32[]{:S(2)}, u32[]{:S(2)}) collective-permute-start(bf16[7,384,128]{2,1,0:T(8,128)(2,1)S(1)} %pad_maximum_fusion.1), channel_id=1, source_target_pairs={{4,0},{8,4},{12,8},{16,12},{20,16},{24,20},{28,24},{0,28},{5,1},{9... | collective-permute-start | bytes 2064392 | tf_op jit(solution)/shard_map/ppermute | solution.py:365
  42.4 8.3 %copy-start.5 = (bf16[18,96,128]{2,1,0:T(8,128)(2,1)S(1)}, bf16[18,96,128]{2,1,0:T(8,128)(2,1)}, u32[]{:S(2)}) copy-start(bf16[18,96,128]{2,1,0:T(8,128)(2,1)} %pack.10) | copy-start | bytes 1327108
  42.4 10.3 %copy-start.4 = (bf16[18,96,128]{2,1,0:T(8,128)(2,1)S(1)}, bf16[18,96,128]{2,1,0:T(8,128)(2,1)}, u32[]{:S(2)}) copy-start(bf16[18,96,128]{2,1,0:T(8,128)(2,1)} %pack.11) | copy-start | bytes 1327108
  43.4 34.9 %copy-start = (bf16[18,96,128]{2,1,0:T(8,128)(2,1)S(1)}, bf16[18,96,128]{2,1,0:T(8,128)(2,1)}, u32[]{:S(2)}) copy-start(bf16[18,96,128]{2,1,0:T(8,128)(2,1)} %pack.8.refs_0_) | copy-start | bytes 1327108
  43.4 30.5 %collective-permute-start.3 = (bf16[18,96,128]{2,1,0:T(8,128)(2,1)S(1)}, bf16[18,96,128]{2,1,0:T(8,128)(2,1)S(1)}, u32[]{:S(2)}, u32[]{:S(2)}) collective-permute-start(bf16[18,96,128]{2,1,0:T(8,128)(2,1)S(1)} %copy-done.6), channel_id=1, source_target_pairs={{0,1},{1,2},{2,3},{3,0},{4,5},{5,6},{6,7},{7,4},{8,9},{9,10},{10,1... | collective-permute-start | bytes 1327112 | tf_op jit(solution)/shard_map/ppermute | solution.py:359
  50.7 27.2 %collective-permute-start.4 = (bf16[18,96,128]{2,1,0:T(8,128)(2,1)S(1)}, bf16[18,96,128]{2,1,0:T(8,128)(2,1)S(1)}, u32[]{:S(2)}, u32[]{:S(2)}) collective-permute-start(bf16[18,96,128]{2,1,0:T(8,128)(2,1)S(1)} %copy-done.5), channel_id=1, source_target_pairs={{0,2},{1,3},{2,0},{3,1},{4,6},{5,7},{6,4},{7,5},{8,10},{9,11},{10,... | collective-permute-start | bytes 1327112 | tf_op jit(solution)/shard_map/ppermute | solution.py:359
  52.7 25.6 %collective-permute-start.5 = (bf16[18,96,128]{2,1,0:T(8,128)(2,1)S(1)}, bf16[18,96,128]{2,1,0:T(8,128)(2,1)S(1)}, u32[]{:S(2)}, u32[]{:S(2)}) collective-permute-start(bf16[18,96,128]{2,1,0:T(8,128)(2,1)S(1)} %copy-done.4), channel_id=1, source_target_pairs={{0,3},{1,0},{2,1},{3,2},{4,7},{5,4},{6,5},{7,6},{8,11},{9,8},{10,9... | collective-permute-start | bytes 1327112 | tf_op jit(solution)/shard_map/ppermute | solution.py:359
  73.9 4.5 %copy-start.3 = (bf16[16,96,128]{2,1,0:T(8,128)(2,1)}, bf16[16,96,128]{2,1,0:T(8,128)(2,1)S(1)}, u32[]{:S(2)}) copy-start(bf16[16,96,128]{2,1,0:T(8,128)(2,1)S(1)} %get-tuple-element.25.refs_0_) | copy-start | bytes 1179652
  78.5 18.0 %collective-permute-start.8 = (bf16[7,384,128]{2,1,0:T(8,128)(2,1)S(1)}, bf16[7,384,128]{2,1,0:T(8,128)(2,1)S(1)}, u32[]{:S(2)}, u32[]{:S(2)}) collective-permute-start(bf16[7,384,128]{2,1,0:T(8,128)(2,1)S(1)} %pad_maximum_fusion.2), channel_id=1, source_target_pairs={{0,4},{4,8},{8,12},{12,16},{16,20},{20,24},{24,28},{28,0},{1,5},{5... | collective-permute-start | bytes 2064392 | tf_op jit(solution)/shard_map/ppermute | solution.py:364
  78.6 17.9 %collective-permute-start.9 = (bf16[7,384,128]{2,1,0:T(8,128)(2,1)S(1)}, bf16[7,384,128]{2,1,0:T(8,128)(2,1)S(1)}, u32[]{:S(2)}, u32[]{:S(2)}) collective-permute-start(bf16[7,384,128]{2,1,0:T(8,128)(2,1)S(1)} %pad_maximum_fusion.3), channel_id=1, source_target_pairs={{4,0},{8,4},{12,8},{16,12},{20,16},{24,20},{28,24},{0,28},{5,1},{9... | collective-permute-start | bytes 2064392 | tf_op jit(solution)/shard_map/ppermute | solution.py:365
  81.3 48.3 %collective-permute-start.13 = (bf16[16,96,128]{2,1,0:T(8,128)(2,1)S(1)}, bf16[16,96,128]{2,1,0:T(8,128)(2,1)S(1)}, u32[]{:S(2)}, u32[]{:S(2)}) collective-permute-start(bf16[16,96,128]{2,1,0:T(8,128)(2,1)S(1)} %get-tuple-element.26), channel_id=1, source_target_pairs={{0,3},{1,0},{2,1},{3,2},{4,7},{5,4},{6,5},{7,6},{8,11},{9,8},{10,9... | collective-permute-start | bytes 1179656 | tf_op jit(solution)/shard_map/ppermute | solution.py:370
  95.9 34.2 %collective-permute-start.14 = (bf16[16,96,128]{2,1,0:T(8,128)(2,1)S(1)}, bf16[16,96,128]{2,1,0:T(8,128)(2,1)S(1)}, u32[]{:S(2)}, u32[]{:S(2)}) collective-permute-start(bf16[16,96,128]{2,1,0:T(8,128)(2,1)S(1)} %get-tuple-element.27), channel_id=1, source_target_pairs={{0,2},{1,3},{2,0},{3,1},{4,6},{5,7},{6,4},{7,5},{8,10},{9,11},{10,... | collective-permute-start | bytes 1179656 | tf_op jit(solution)/shard_map/ppermute | solution.py:370
  95.9 34.2 %collective-permute-start.15 = (bf16[16,96,128]{2,1,0:T(8,128)(2,1)S(1)}, bf16[16,96,128]{2,1,0:T(8,128)(2,1)}, u32[]{:S(2)}, u32[]{:S(2)}) collective-permute-start(bf16[16,96,128]{2,1,0:T(8,128)(2,1)S(1)} %get-tuple-element.28), channel_id=1, source_target_pairs={{0,1},{1,2},{2,3},{3,0},{4,5},{5,6},{6,7},{7,4},{8,9},{9,10},{10,1... | collective-permute-start | bytes 1179656 | tf_op jit(solution)/shard_map/ppermute | solution.py:370
  115.1 23.7 %collective-permute-start.10 = (bf16[16,96,128]{2,1,0:T(8,128)(2,1)S(1)}, bf16[16,96,128]{2,1,0:T(8,128)(2,1)S(1)}, u32[]{:S(2)}, u32[]{:S(2)}) collective-permute-start(bf16[16,96,128]{2,1,0:T(8,128)(2,1)S(1)} %get-tuple-element.34), channel_id=1, source_target_pairs={{0,3},{1,0},{2,1},{3,2},{4,7},{5,4},{6,5},{7,6},{8,11},{9,8},{10,9... | collective-permute-start | bytes 1179656 | tf_op jit(solution)/shard_map/ppermute | solution.py:370
  129.6 33.8 %collective-permute-start.11 = (bf16[16,96,128]{2,1,0:T(8,128)(2,1)S(1)}, bf16[16,96,128]{2,1,0:T(8,128)(2,1)S(1)}, u32[]{:S(2)}, u32[]{:S(2)}) collective-permute-start(bf16[16,96,128]{2,1,0:T(8,128)(2,1)S(1)} %get-tuple-element.35), channel_id=1, source_target_pairs={{0,2},{1,3},{2,0},{3,1},{4,6},{5,7},{6,4},{7,5},{8,10},{9,11},{10,... | collective-permute-start | bytes 1179656 | tf_op jit(solution)/shard_map/ppermute | solution.py:370
  129.6 33.8 %collective-permute-start.12 = (bf16[16,96,128]{2,1,0:T(8,128)(2,1)S(1)}, bf16[16,96,128]{2,1,0:T(8,128)(2,1)S(1)}, u32[]{:S(2)}, u32[]{:S(2)}) collective-permute-start(bf16[16,96,128]{2,1,0:T(8,128)(2,1)S(1)} %get-tuple-element.36), channel_id=1, source_target_pairs={{0,1},{1,2},{2,3},{3,0},{4,5},{5,6},{6,7},{7,4},{8,9},{9,10},{10,1... | collective-permute-start | bytes 1179656 | tf_op jit(solution)/shard_map/ppermute | solution.py:370
  138.9 24.5 %copy-start.7 = (bf16[16,96,128]{2,1,0:T(8,128)(2,1)}, bf16[16,96,128]{2,1,0:T(8,128)(2,1)S(1)}, u32[]{:S(2)}) copy-start(bf16[16,96,128]{2,1,0:T(8,128)(2,1)S(1)} %collective-permute-done.10.refs_1_) | copy-start | bytes 1179652
  (9 other events, 11.7 us)
